TPU v7x, 32 devices: a whole 2x2x4 slice. The times are simulated.
32 devices in a mesh: seq: 8 (over y, x, core), head: 4 (over z).
Axes of the slice: x: 2, y: 2, z: 4, core: 2. Of those that a mesh axis runs over, the one named last changes fastest.
Arguments:
- x_in: bfloat16 [2048, 8192], P('seq', 'head'), may hold values from -6 to 6
- b_in: bfloat16 [2048, 128], P(('seq', 'head')), may hold values from -0.625 to 0.625
- c_in: bfloat16 [2048, 128], P(('seq', 'head')), may hold values from -0.625 to 0.625
- decay_codes: int32 [128, 2048], P('head', 'seq'), may hold values from 0 to 7168
- decay_rate: float32 [128], P('head'), may hold values from 0 to 0.05
- skip_gain: float32 [128], P('head'), may hold values from 0.5 to 1.5
- out_grad: bfloat16 [2048, 8192], P('seq', 'head'), may hold values from -6 to 6
Outputs:
- ssm_out: bfloat16 [2048, 8192], P('seq', 'head')
- input_grad: bfloat16 [2048, 8192], P('seq', 'head')
- grad_b: float32 [2048, 128], P(('seq', 'head'))
- grad_c: float32 [2048, 128], P(('seq', 'head'))
All inputs are finite; a program needn't handle non-finite values.
Results may differ from a plain program's by a relative error of at most 0.005.
Values may be sent and summed in bfloat16 or wider, within the bound.
A program may use at most 64 MiB of HBM per device.

v0:
```python
import jax
import jax.numpy as jnp
from jax import lax
from jax.sharding import PartitionSpec as P

HEAD_DIM = 64
STATE = 128
BLOCK = 256


def carried_in(x, axis, combine, identity, reverse):
    size, place = (lax.axis_size(axis), lax.axis_index(axis))
    everything = jax.tree.map(lambda part: lax.all_gather(part, axis), x)
    start = jax.tree.map(
        lambda part, zero: jnp.broadcast_to(jnp.asarray(zero, part.dtype), part.shape), x, identity
    )

    def hop(k, before):
        at = size - 1 - k if reverse else k
        reached = at > place if reverse else at < place
        new = combine(before, jax.tree.map(lambda part: part[at], everything))
        return jax.tree.map(lambda a, b: jnp.where(reached, a, b), new, before)

    return lax.fori_loop(0, size, hop, start)


def exact(form, operands):
    return jnp.einsum(form, *operands, precision=lax.Precision.HIGHEST)


def decode(decay_labels, decay_speeds):
    time_delta = 0.5 + (decay_labels % 1024).astype(jnp.float32) / 1024.0
    spike_loss_term = 0.1 * (decay_labels // 1024).astype(jnp.float32)
    return (time_delta, -decay_speeds[:, None] * time_delta - spike_loss_term)


def summarize(cumul, b_block, c_block, driven, cotangent):
    tail = jnp.exp(cumul[:, -1:] - cumul)
    state_part = exact("hj,jn,jhp->hpn", (tail, b_block.astype(jnp.float32), driven))
    adjoint_part = exact("hi,in,ihp->hpn", (jnp.exp(cumul), c_block.astype(jnp.float32), cotangent))
    return (state_part, adjoint_part)


def within(cumul, b_block, c_block, driven_low, cot_low):
    width = cumul.shape[1]
    causal = lax.broadcasted_iota(jnp.int32, (width, width), 0) >= lax.broadcasted_iota(
        jnp.int32, (width, width), 1
    )
    spread = cumul[:, :, None] - cumul[:, None, :]
    weights = jnp.where(causal, jnp.exp(jnp.where(causal, spread, 0.0)), 0.0)
    scores = jnp.dot(c_block, b_block.T, preferred_element_type=jnp.float32)
    mixed = (weights * scores).astype(jnp.bfloat16)
    out_part = jnp.einsum("hij,jhp->ihp", mixed, driven_low, preferred_element_type=jnp.float32)
    drive_grad = jnp.einsum("hij,ihp->jhp", mixed, cot_low, preferred_element_type=jnp.float32)
    pair_raw = jnp.einsum("ihp,jhp->hij", cot_low, driven_low, preferred_element_type=jnp.float32)
    paired = (weights * pair_raw).astype(jnp.bfloat16)
    c_grad = jnp.einsum("hij,jn->in", paired, b_block, preferred_element_type=jnp.float32)
    b_grad = jnp.einsum("hij,in->jn", paired, c_block, preferred_element_type=jnp.float32)
    return (out_part, drive_grad, c_grad, b_grad)


def summarize_group(group):
    return summarize(group[0], group[1], group[2], group[3], group[4])


def within_group(group):
    return within(group[0], group[1], group[2], group[5], group[6])


def both_group(group):
    return summarize_group(group) + within_group(group)


def link(before_part, after_part):
    return (
        before_part[0] + after_part[0],
        jnp.exp(after_part[0])[:, None, None] * before_part[1] + after_part[1],
    )


def advance(running, element):
    contrib, totals = element
    return (jnp.exp(totals)[:, None, None] * running + contrib, running)


def carries(state_parts, adjoint_parts, totals):
    head_count = totals.shape[1]
    blank_state = jnp.zeros(state_parts.shape[1:], jnp.float32)
    state_total, entering = lax.scan(advance, blank_state, (state_parts, totals))
    adjoint_total, outgoing_state = lax.scan(
        advance, blank_state, (adjoint_parts, totals), reverse=True
    )
    decay_total = jnp.sum(totals, axis=0)
    identity = (jnp.zeros((head_count,), jnp.float32), blank_state)
    state_in = carried_in((decay_total, state_total), "seq", link, identity, False)[1]
    adjoint_in = carried_in((decay_total, adjoint_total), "seq", link, identity, True)[1]
    running_sum = jnp.cumsum(totals, axis=0)
    before_sum = running_sum - totals
    after_sum = decay_total[None, :] - running_sum
    full_states = entering + jnp.exp(before_sum)[:, :, None, None] * state_in[None]
    full_adjoints = outgoing_state + jnp.exp(after_sum)[:, :, None, None] * adjoint_in[None]
    return (full_states, full_adjoints)


def local(x_in, b_in, c_in, decay_codes, decay_rate, skip_gain, out_grad):
    head_count = decay_rate.shape[0]
    token_count = x_in.shape[0]
    blocks = token_count // BLOCK
    b_full, output_matrix_full = (
        lax.all_gather(b_in, "head", axis=0, tiled=True),
        lax.all_gather(c_in, "head", axis=0, tiled=True),
    )
    time_delta, log_decay = decode(decay_codes, decay_rate)
    inputs = x_in.astype(jnp.float32).reshape(blocks, BLOCK, head_count, HEAD_DIM)
    cot_low = out_grad.reshape(blocks, BLOCK, head_count, HEAD_DIM)
    cotangent = cot_low.astype(jnp.float32)
    step_tokens = time_delta.reshape(head_count, blocks, BLOCK).transpose(1, 2, 0)[..., None]
    driven_low = (inputs * step_tokens).astype(jnp.bfloat16)
    driven = driven_low.astype(jnp.float32)
    cumul = jnp.cumsum(log_decay.reshape(head_count, blocks, BLOCK), axis=2).transpose(1, 0, 2)
    totals = cumul[:, :, -1]
    input_matrix_blocks = b_full.reshape(blocks, BLOCK, STATE)
    c_blocks = output_matrix_full.reshape(blocks, BLOCK, STATE)
    operands = (cumul, input_matrix_blocks, c_blocks, driven, cotangent, driven_low, cot_low)
    state_parts, adjoint_parts, out_part, drive_grad, c_grad, b_grad = lax.map(both_group, operands)
    full_states, full_adjoints = carries(state_parts, adjoint_parts, totals)
    growth = jnp.exp(cumul)
    tail = jnp.exp(totals[:, :, None] - cumul)
    c_wide = c_blocks.astype(jnp.float32)
    b_wide = input_matrix_blocks.astype(jnp.float32)
    out_cross = exact("khi,khpn,kin->kihp", (growth, full_states, c_wide))
    c_cross = exact("khi,kihp,khpn->kin", (growth, cotangent, full_states))
    drive_cross = exact("khj,khpn,kjn->kjhp", (tail, full_adjoints, b_wide))
    b_cross = exact("khj,kjhp,khpn->kjn", (tail, driven, full_adjoints))
    gain = skip_gain[None, None, :, None]
    ssm_out = (out_part + out_cross + gain * inputs).astype(jnp.bfloat16)
    ssm_out = ssm_out.reshape(token_count, head_count * HEAD_DIM)
    input_grad = (gain * cotangent + step_tokens * (drive_grad + drive_cross)).astype(jnp.bfloat16)
    input_grad = input_grad.reshape(token_count, head_count * HEAD_DIM)
    b_sum = (b_grad + b_cross).reshape(token_count, STATE)
    c_sum = (c_grad + c_cross).reshape(token_count, STATE)
    grad_b, grad_c = (
        lax.psum_scatter(b_sum, "head", scatter_dimension=0, tiled=True),
        lax.psum_scatter(c_sum, "head", scatter_dimension=0, tiled=True),
    )
    return (ssm_out, input_grad, grad_b, grad_c)


def solution(mesh):
    placed = (
        P("seq", "head"),
        P(("seq", "head"), None),
        P(("seq", "head"), None),
        P("head", "seq"),
        P("head"),
        P("head"),
        P("seq", "head"),
    )
    return jax.shard_map(
        local,
        mesh=mesh,
        in_specs=placed,
        out_specs=(
            P("seq", "head"),
            P("seq", "head"),
            P(("seq", "head"), None),
            P(("seq", "head"), None),
        ),
        check_vma=False,
    )
```

profile of v0, /device:TPU:0, one launch (start us, length us, event | category | flops | bytes accessed | tf_op | source)
XLA Modules:
  0.0 190.6 jit_solution(5804453868903362087)
XLA Ops:
  10.7 1.5 copy.57
  12.2 14.9 %all_gather.20 = bf16[256,128]{1,0:T(8,128)(2,1)S(1)} all-gather(bf16[64,128]{1,0:T(8,128)(2,1)S(1)} %copy-done.6), channel_id=1, replica_groups=mesh['seq'=8,'head'=4] {'head'}, dimensions={0}, use_global_device_ids=true | all-gather | bytes 81920 | tf_op jit(solution)/shard_map/all_gather | solution.py:111
  27.1 2.1 %fusion.17 = f32[32,64,128]{2,1,0:T(8,128)} fusion(bf16[256,32,64]{0,2,1:T(8,128)(2,1)S(1)} %bitcast.106, f32[256,32]{0,1:T(8,128)S(1)} %get-tuple-element.390, f32[32]{0:T(128)S(1)} %get-tuple-element.395, bf16[256,128]{1,0:T(8,128)(2,1)S(1)} %all_gather.20), kind=kOutput, calls=%fused_computation.32 | convolution fusion | flops 806617088 | bytes 2195584 | tf_op jit(solution)/shard_map/while/body/eval_jaxpr/hi,in,ihp->hpn/dot_general | solution.py:28
  29.3 1.5 copy.49
  30.8 13.3 %all_gather.21 = bf16[256,128]{1,0:T(8,128)(2,1)S(1)} all-gather(bf16[64,128]{1,0:T(8,128)(2,1)S(1)} %copy-done.7), channel_id=1, replica_groups=mesh['seq'=8,'head'=4] {'head'}, dimensions={0}, use_global_device_ids=true | all-gather | bytes 81920 | tf_op jit(solution)/shard_map/all_gather | solution.py:110
  44.2 2.1 %fusion.16 = f32[32,64,128]{2,1,0:T(8,128)} fusion(f32[256,32]{0,1:T(8,128)S(1)} %get-tuple-element.391, f32[32]{0:T(128)S(1)} %get-tuple-element.395, f32[256,32,64]{0,2,1:T(8,128)S(1)} %bitcast.102, f32[256,32]{0,1:T(8,128)S(1)} %get-tuple-element.392, bf16[256,128]{1,0:T(8,128)(2,1)S(1)} %all_gather.21), kind=kOutput, calls=%fused_computation.31 | convolution fusion | flops 807665664 | bytes 3276928 | tf_op jit(solution)/shard_map/while/body/eval_jaxpr/hj,jn,jhp->hpn/dot_general | solution.py:28
  46.5 8.7 %all-gather = f32[8,32,1]{1,2,0:T(1,128)S(1)} all-gather(f32[1,32,1]{1,2,0:T(1,128)S(1)} %copy.56), channel_id=2, replica_groups=mesh['seq'=8,'head'=4] {'seq'}, dimensions={0}, use_global_device_ids=true | all-gather | bytes 1152 | tf_op jit(solution)/shard_map/all_gather | solution.py:13
  56.2 4.3 %convert_reduce_fusion = bf16[256,256]{0,1:T(8,128)(2,1)S(1)} fusion(f32[32,256]{1,0:T(8,128)S(1)} %get-tuple-element.387, pred[256,256]{0,1:T(8,128)(4,1)S(1)} %iota_compare_fusion, bf16[256,32,64]{0,2,1:T(8,128)(2,1)S(1)} %bitcast.107, f32[256,32,64]{0,2,1:T(8,128)} %bitcast.103, f32[256,32]{0,1:T(8,128)S(1)} %get-tuple-element.392), kind=kOutput, calls=%fused_computation.8 | convolution fusion | flops 284098560 | bytes 3407872 | tf_op jit(solution)/shard_map/while/body/eval_jaxpr/ihp,jhp->hij/dot_general | solution.py:55
  60.5 24.5 %all-gather.8.cloned.1.call-done = f32[256,64,128]{2,1,0:T(8,128)} async-done(((f32[32,64,128]{2,1,0:T(8,128)}), f32[256,64,128]{2,1,0:T(8,128)}) %all-gather.8.cloned.1.call-update) | async-done | bytes 8388624 | tf_op jit(solution)/shard_map/all_gather | solution.py:13
  85.0 12.3 %while.21 = (s32[]{:T(128)}, f32[32,64,128]{2,1,0:T(8,128)S(1)}, s32[]{:T(128)}, f32[8,32]{1,0:T(8,128)S(1)}, f32[8,32,64,128]{3,2,1,0:T(8,128)}, /*index=5*/s32[]{:T(128)}, s32[]{:T(128)}, s32[]{:T(128)}, s32[]{:T(128)}) while((s32[]{:T(128)}, f32[32,64,128]{2,1,0:T(8,128)S(1)}, s32[]{:T(128)}, f32[8,32]{1,0:T(8,128)S(1)}, ...), condition=%wide.region_5.6_spmd.clone, body=%wide.region_4.5_spmd.clone.sunk | while | flops 1048584 | bytes 3146279 | solution.py:24
  86.5 1.5 fusion.62
  92.5 1.5 fusion.62
  94.1 1.6 fusion.62
  95.7 1.5 fusion.62
  97.3 5.1 %fusion.18 = f32[256,128]{1,0:T(8,128)S(1)} fusion(f32[256,32]{0,1:T(8,128)S(1)} %get-tuple-element.386, f32[32,64,128]{2,1,0:T(8,128)S(1)} %get-tuple-element.303, f32[32]{0:T(128)S(1)} %get-tuple-element.394, f32[256,32,64]{0,2,1:T(8,128)} %bitcast.104, f32[256,32]{0,1:T(8,128)S(1)} %get-tuple-element.392), kind=kOutput, calls=%fused_computation.33 | convolution fusion | flops 807665664 | bytes 3342464 | tf_op jit(solution)/shard_map/khj,kjhp,khpn->kjn/dot_general | solution.py:28
  103.2 2.4 %fusion.25 = f32[32,64,256]{2,1,0:T(8,128)} fusion(f32[32,64,128]{2,1,0:T(8,128)S(1)} %get-tuple-element.303, f32[32]{0:T(128)S(1)} %get-tuple-element.394, bf16[256,128]{1,0:T(8,128)(2,1)S(1)} %all_gather.21), kind=kOutput, calls=%fused_computation.42 | convolution fusion | flops 805568512 | bytes 3211392 | tf_op jit(solution)/shard_map/khj,khpn,kjn->kjhp/dot_general | solution.py:28
  105.8 36.0 %all-gather.6.cloned.1.call-done = f32[256,64,128]{2,1,0:T(8,128)} async-done(((f32[32,64,128]{2,1,0:T(8,128)}), f32[256,64,128]{2,1,0:T(8,128)}) %all-gather.6.cloned.1.call-update) | async-done | bytes 8388624 | tf_op jit(solution)/shard_map/all_gather | solution.py:13
  141.8 12.0 %while.20 = (s32[]{:T(128)}, f32[32,64,128]{2,1,0:T(8,128)S(1)}, s32[]{:T(128)}, f32[8,32]{1,0:T(8,128)S(1)}, f32[8,32,64,128]{3,2,1,0:T(8,128)}, /*index=5*/s32[]{:T(128)}, s32[]{:T(128)}) while((s32[]{:T(128)}, f32[32,64,128]{2,1,0:T(8,128)S(1)}, s32[]{:T(128)}, f32[8,32]{1,0:T(8,128)S(1)}, f32[8,32,64,128]{3,2,1,0:T(8,128)}, ...), condition=%wide.region_3.4_spmd.clone, body=%wide.region_2.3_spmd.clone.sunk | while | flops 1048580 | bytes 3146217 | solution.py:24
  150.9 1.5 fusion.61
  153.8 2.3 %fusion.28 = f32[32,64,256]{2,1,0:T(8,128)} fusion(f32[32,64,128]{2,1,0:T(8,128)S(1)} %get-tuple-element.302, f32[32]{0:T(128)S(1)} %get-tuple-element.394, bf16[256,128]{1,0:T(8,128)(2,1)S(1)} %all_gather.20), kind=kOutput, calls=%fused_computation.45 | convolution fusion | flops 805568512 | bytes 3211392 | tf_op jit(solution)/shard_map/khi,khpn,kin->kihp/dot_general | solution.py:28
  156.2 3.5 %fusion.19 = f32[256,128]{1,0:T(8,128)S(1)} fusion(bf16[256,32,64]{0,2,1:T(8,128)(2,1)S(1)} %bitcast.108, f32[256,32]{0,1:T(8,128)S(1)} %get-tuple-element.390, f32[32,64,128]{2,1,0:T(8,128)S(1)} %get-tuple-element.302, f32[32]{0:T(128)S(1)} %get-tuple-element.394), kind=kOutput, calls=%fused_computation.34 | convolution fusion | flops 806617088 | bytes 2261120 | tf_op jit(solution)/shard_map/khi,kihp,khpn->kin/dot_general | solution.py:28
  160.7 4.6 %fusion.10 = bf16[256,32,64]{0,2,1:T(8,128)(2,1)S(1)} fusion(bf16[256,32,64]{0,2,1:T(8,128)(2,1)S(1)} %bitcast.109, f32[32,64,256]{2,1,0:T(8,128)} %fusion.25, f32[256,256]{0,1:T(8,128)S(1)} %copy-done.3, f32[32,256]{1,0:T(8,128)S(1)} %get-tuple-element.387, pred[256,256]{0,1:T(8,128)(4,1)S(1)} %copy-done.5, f32[256,32]{0,1:T(8,128)S(1)} %get-tuple-element.386, ...), kind=kOutput, calls=%fused_computation.22 | convolution fusion | flops 282591232 | bytes 4620416 | tf_op jit(solution)/shard_map/while/body/eval_jaxpr/hij,ihp->jhp/dot_general | solution.py:54
  165.3 3.0 %fusion.15 = bf16[256,32,64]{0,2,1:T(8,128)(2,1)S(1)} fusion(f32[32,64,256]{2,1,0:T(8,128)S(1)} %copy-done.2, f32[256,32,64]{0,2,1:T(8,128)S(1)} %bitcast.105, f32[256,256]{0,1:T(8,128)S(1)} %copy-done.3, f32[32,256]{1,0:T(8,128)S(1)} %get-tuple-element.387, pred[256,256]{0,1:T(8,128)(4,1)S(1)} %copy-done.5, f32[32]{0:T(128)S(1)} %copy-done.8, ...), kind=kOutput, calls=%fused_computation.29 | convolution fusion | flops 282591232 | bytes 5668992 | tf_op jit(solution)/shard_map/while/body/eval_jaxpr/hij,jhp->ihp/dot_general | solution.py:53
  171.2 12.8 %reduce-scatter.5.cloned.1.call-done = f32[64,128]{1,0:T(8,128)} async-done(((f32[256,128]{1,0:T(8,128)}), f32[64,128]{1,0:T(8,128)}) %reduce-scatter.5.cloned.1.call-update) | async-done | bytes 32784 | tf_op jit(solution)/shard_map/reduce_scatter | solution.py:144
  (80 shorter events, 25.7 us)
Async XLA Ops:
  7.2 5.1 %copy-start.6 = (bf16[64,128]{1,0:T(8,128)(2,1)S(1)}, bf16[64,128]{1,0:T(8,128)(2,1)}, u32[]{:S(2)}) copy-start(bf16[64,128]{1,0:T(8,128)(2,1)} %param.13) | copy-start | bytes 49156
  7.2 77.8 %all-gather.8.cloned.1.call-start = ((), (), s32[]{:S(2)}) async-start(), calls=%async_computation.5 | async-start | bytes 9437184 | tf_op jit(solution)/shard_map/all_gather | solution.py:13
  29.3 1.6 copy-start.7
  29.3 112.6 %all-gather.6.cloned.1.call-start = ((), (), s32[]{:S(2)}) async-start(), calls=%async_computation.4 | async-start | bytes 9437184 | tf_op jit(solution)/shard_map/all_gather | solution.py:13
  30.8 15.5 %copy-start = (f32[256,2048]{0,1:T(8,128)}, f32[256,2048]{0,1:T(8,128)S(1)}, u32[]{:S(2)}) copy-start(f32[256,2048]{0,1:T(8,128)S(1)} %copy.49) | copy-start | bytes 6291460
  46.4 124.8 %reduce-scatter.3.cloned.1.call-start = ((), (), s32[]{:S(2)}) async-start(), calls=%async_computation.2 | async-start | bytes 163840 | tf_op jit(solution)/shard_map/reduce_scatter | solution.py:143
  55.3 0.9 copy-start.4
  105.6 78.4 %reduce-scatter.5.cloned.1.call-start = ((), (), s32[]{:S(2)}) async-start(), calls=%async_computation.3 | async-start | bytes 163840 | tf_op jit(solution)/shard_map/reduce_scatter | solution.py:144
  156.2 4.5 %copy-start.3 = (f32[256,256]{0,1:T(8,128)S(1)}, f32[256,256]{0,1:T(8,128)}, u32[]{:S(2)}) copy-start(f32[256,256]{0,1:T(8,128)} %fusion.50) | copy-start | bytes 786436
  156.2 4.5 %copy-start.5 = (pred[256,256]{0,1:T(8,128)(4,1)S(1)}, pred[256,256]{0,1:T(8,128)(4,1)}, u32[]{:S(2)}) copy-start(pred[256,256]{0,1:T(8,128)(4,1)} %copy-done.4) | copy-start | bytes 196612
  156.2 4.5 %copy-start.8 = (f32[32]{0:T(128)S(1)}, f32[32]{0:T(128)}, u32[]{:S(2)}) copy-start(f32[32]{0:T(128)} %param.16) | copy-start | bytes 388
  160.7 4.6 %copy-start.1 = (f32[256,2048]{0,1:T(8,128)S(1)}, f32[256,2048]{0,1:T(8,128)}, u32[]{:S(2)}) copy-start(f32[256,2048]{0,1:T(8,128)} %copy-done) | copy-start | bytes 6291460
  160.7 4.6 %copy-start.2 = (f32[32,64,256]{2,1,0:T(8,128)S(1)}, f32[32,64,256]{2,1,0:T(8,128)}, u32[]{:S(2)}) copy-start(f32[32,64,256]{2,1,0:T(8,128)} %fusion.28) | copy-start | bytes 6291460
Sparse Core Ops, SparseCore 0:
  29.4 55.5 all-gather.7
  87.4 54.3 all-gather.5
  144.7 19.1 reduce-scatter.2
  166.7 17.3 reduce-scatter.4
where the time goes:
time: 192 us; the launch traced here: 191 us
  waiting for transfers between devices  73.4 us (38%)
  blocking collectives  37 us (19%)
  matrix products  32.2 us (17%)
  other arithmetic  26.5 us (14%)
  between operations  14 us (7%)
  local copies, waits for them, and re-layouts  6.68 us (3%)
    all_gather x2, waiting for transfers between devices, carried_in(): everything = jax.tree.map(lambda part: lax.all_gather(part, axis), x)  60.5 us
    select_n x16, other arithmetic, hop(): return jax.tree.map(lambda a, b: jnp.where(reached, a, b), new, before)  23.6 us
    dot_general x6, matrix products, exact(): return jnp.einsum(form, *operands, precision=lax.Precision.HIGHEST)  17.7 us
    all_gather x1, blocking collectives, local(): lax.all_gather(c_in, 'head', axis=0, tiled=True)  14.9 us
    all_gather x1, blocking collectives, local(): lax.all_gather(b_in, 'head', axis=0, tiled=True)  13.3 us
    reduce_scatter x1, waiting for transfers between devices, local(): lax.psum_scatter(c_sum, 'head', scatter_dimension=0, tiled=True)  12.8 us
    all_gather x1, blocking collectives, carried_in(): everything = jax.tree.map(lambda part: lax.all_gather(part, axis), x)  8.75 us
    dot_general x1, matrix products, within(): jnp.einsum('hij,ihp->jhp', mixed, cot_low, preferred_element_type=jnp.flo...  4.61 us
  transfers between devices with their start and end apart: 4, of which 3 were waited for; matrix products, arithmetic and copies ran while one was open for 31% of the time, Pallas kernels for 0%

commit v1 on v0

v1 whole, which is shorter than its diff:
```python
import functools

import jax
import jax.numpy as jnp
from jax import lax
from jax.experimental import pallas as pl
from jax.experimental.pallas import tpu as pltpu
from jax.sharding import PartitionSpec as P

SUB = 128
MESH = pl.DeviceIdType.MESH
F32 = jnp.float32
BF16 = jnp.bfloat16


def dot(a, b, dims=((1,), (0,))):
    return lax.dot_general(a, b, (dims, ((), ())), preferred_element_type=F32)


def split3(a):
    hi = a.astype(BF16).astype(F32)
    mid = (a - hi).astype(BF16).astype(F32)
    low = a - hi - mid
    return jnp.concatenate([hi, mid, low], axis=0).astype(BF16)


def split_dot(a, b, dims=((1,), (0,))):
    hi = a.astype(BF16)
    low = (a - hi.astype(F32)).astype(BF16)
    return dot(hi, b, dims) + dot(low, b, dims)


def kernel(
    chips, zs,
    x_ref, b_ref, c_ref, codes_ref, rate_ref, gain_ref, g_ref,
    out_ref, ig_ref, gb_ref, gc_ref,
    u_s, vs_s, ug_s, vx_s, od_s, gd_s, ps_s, as_s, gain_s,
    bc, pa, dd, pc, dc, qb, qt, rq, rt, tmp, ef, part, rpart,
    g_send, g_recv, s_send, s_recv, q_send, q_recv, t_send, t_recv, r_send, r_recv,
):
    tokens, width = x_ref.shape
    heads = codes_ref.shape[0]
    dim = width // heads
    state = b_ref.shape[1]
    rows = b_ref.shape[0]
    subs = tokens // SUB
    half = width // 2
    seq = lax.axis_index("seq")
    z = lax.axis_index("head")
    chip = seq // 2
    core = seq % 2
    other = 1 - core
    sib = {"seq": chip * 2 + other, "head": z}

    def z_peer(d):
        return {"seq": seq, "head": (z + d) % zs}

    def chip_peer(d):
        return {"seq": ((chip + d) % chips) * 2 + core, "head": z}

    def copy(src, dst, send, recv, to):
        return pltpu.make_async_remote_copy(
            src_ref=src, dst_ref=dst, send_sem=send, recv_sem=recv,
            device_id=to, device_id_type=MESH,
        )

    barrier = pltpu.get_barrier_semaphore()
    for d in range(1, zs):
        pl.semaphore_signal(barrier, inc=1, device_id=z_peer(d), device_id_type=MESH)
    for d in range(1, chips):
        pl.semaphore_signal(barrier, inc=1, device_id=chip_peer(d), device_id_type=MESH)
    pl.semaphore_signal(barrier, inc=1, device_id=sib, device_id_type=MESH)
    bc[z, 0] = b_ref[...]
    bc[z, 1] = c_ref[...]
    pl.semaphore_wait(barrier, zs + chips - 1)

    gathers = [
        copy(bc.at[z], bc.at[z], g_send.at[d - 1], g_recv.at[d - 1], z_peer(d))
        for d in range(1, zs)
    ]
    for each in gathers:
        each.start()

    eye = lax.broadcasted_iota(jnp.int32, (heads, heads), 0) == lax.broadcasted_iota(
        jnp.int32, (heads, heads), 1
    )
    rate = jnp.sum(jnp.where(eye, rate_ref[...], 0.0), axis=1, keepdims=True)
    gain = jnp.sum(jnp.where(eye, gain_ref[...], 0.0), axis=1, keepdims=True)
    codes = codes_ref[...]
    step = 0.5 + (codes & 1023).astype(F32) * (1.0 / 1024.0)
    log_decay = -rate * step - 0.1 * (codes >> 10).astype(F32)
    at_u = lax.broadcasted_iota(jnp.int32, (tokens, tokens), 0)
    at_t = lax.broadcasted_iota(jnp.int32, (tokens, tokens), 1)
    centred = jnp.where(
        at_u // SUB == at_t // SUB, jnp.where(at_u <= at_t, 0.5, -0.5), 0.0
    ).astype(BF16)
    logs = dot(split3(log_decay), centred)
    logs = logs[:heads] + logs[heads : 2 * heads] + logs[2 * heads :]
    u3 = split3(jnp.exp(logs))
    v3 = split3(jnp.exp(-logs) * step)
    head_of = lax.broadcasted_iota(jnp.int32, (heads, width), 1) // dim
    spread = (head_of == lax.broadcasted_iota(jnp.int32, (heads, width), 0)).astype(F32)
    gain_s[...] = jnp.sum(spread * gain, axis=0, keepdims=True)
    spread3 = jnp.concatenate([spread] * 3, axis=0).astype(BF16)
    u_s[...] = dot(u3, spread3, ((0,), (0,)))
    vs_s[...] = dot(v3, spread3, ((0,), (0,)))
    ug_s[...] = (u_s[...] * g_ref[...].astype(F32)).astype(BF16)
    vx_s[...] = (vs_s[...] * x_ref[...].astype(F32)).astype(BF16)

    for each in gathers:
        each.wait()
    b_all = bc[:, 0].reshape(tokens, state)
    c_all = bc[:, 1].reshape(tokens, state)

    def block(a):
        return slice(a * SUB, (a + 1) * SUB)

    def root(a, lanes):
        return u_s[(a + 1) * SUB - 1 : (a + 1) * SUB, lanes]

    halves = [slice(0, half), slice(half, width)]
    for h, lanes in enumerate(halves):
        total = None
        for a in range(subs):
            r = root(a, lanes)
            ps = r * dot(b_all[block(a)], vx_s[block(a), lanes], ((0,), (0,)))
            ad = r * dot(c_all[block(a)], ug_s[block(a), lanes], ((0,), (0,)))
            ps_s[a, :, lanes] = ps
            as_s[a, :, lanes] = ad
            if a == 0:
                p_dev, a_dev, total = ps, ad, r * r
            else:
                p_dev = (r * r) * p_dev + ps
                a_dev = a_dev + total * ad
                total = total * (r * r)
        pa[h, 0] = p_dev.astype(BF16)
        pa[h, 1] = a_dev.astype(BF16)
        dd[h] = total

    to_sib = [
        copy(pa.at[other], pc.at[core], s_send.at[0], s_recv.at[0], sib),
        copy(dd.at[other], dc.at[core], s_send.at[1], s_recv.at[1], sib),
    ]
    for each in to_sib:
        each.start()
    pc[core] = pa[core]
    dc[core] = dd[core]
    for each in to_sib:
        each.wait()
    p0, p1 = pc[0, 0].astype(F32), pc[1, 0].astype(F32)
    a0, a1 = pc[0, 1].astype(F32), pc[1, 1].astype(F32)
    qb[0] = (dc[1] * p0 + p1).astype(BF16)
    qb[1] = (a0 + dc[0] * a1).astype(BF16)
    qt[...] = dc[0] * dc[1]
    to_chips = []
    for d in range(1, chips):
        kind = (chip + d) // chips
        to_chips.append(
            copy(qb.at[kind], rq.at[d - 1], q_send.at[d - 1], q_recv.at[d - 1], chip_peer(d))
        )
        to_chips.append(
            copy(qt, rt.at[d - 1], t_send.at[d - 1], t_recv.at[d - 1], chip_peer(d))
        )
    for each in to_chips:
        each.start()

    at_r = lax.broadcasted_iota(jnp.int32, (SUB, SUB), 0)
    at_c = lax.broadcasted_iota(jnp.int32, (SUB, SUB), 1)
    sums = []
    for a in range(subs):
        b_a, c_a = b_all[block(a)], c_all[block(a)]
        scores = jnp.where(at_r >= at_c, dot(c_a, b_a, ((1,), (1,))), 0.0).astype(BF16)
        flipped = jnp.where(at_r <= at_c, dot(b_a, c_a, ((1,), (1,))), 0.0).astype(BF16)
        od_s[block(a)] = dot(scores, vx_s[block(a)])
        gd_s[block(a)] = dot(flipped, ug_s[block(a)])
        paired = dot(ug_s[block(a)], vx_s[block(a)], ((1,), (1,)))
        paired = jnp.where(at_r >= at_c, paired, 0.0)
        sums.append((split_dot(paired.T, c_a), split_dot(paired, b_a)))

    for each in to_chips:
        each.wait()
    e_in = jnp.zeros((state, half), F32)
    f_in = jnp.zeros((state, half), F32)
    reach = jnp.ones((1, half), F32)
    for d in range(1, chips):
        e_in = e_in + jnp.where(chip >= d, reach, 0.0) * rq[d - 1].astype(F32)
        reach = reach * rt[d - 1]
    reach = jnp.ones((1, half), F32)
    for d in range(chips - 1, 0, -1):
        f_in = f_in + jnp.where(chip < d, reach, 0.0) * rq[d - 1].astype(F32)
        reach = reach * rt[d - 1]
    tmp[0, 0] = e_in.astype(BF16)
    tmp[1, 0] = (dc[0] * e_in + pc[0, 0].astype(F32)).astype(BF16)
    tmp[1, 1] = f_in.astype(BF16)
    tmp[0, 1] = (dc[1] * f_in + pc[1, 1].astype(F32)).astype(BF16)
    back = copy(tmp.at[other], ef.at[core], s_send.at[2], s_recv.at[2], sib)
    back.start()
    ef[core] = tmp[core]
    back.wait()

    states = {}
    for h, lanes in enumerate(halves):
        e = ef[h, 0].astype(F32)
        f = ef[h, 1].astype(F32)
        for a in range(subs):
            r = root(a, lanes)
            states[h, a, 0] = (r * e).astype(BF16)
            e = (r * r) * e + ps_s[a, :, lanes]
        for a in range(subs - 1, -1, -1):
            r = root(a, lanes)
            states[h, a, 1] = (r * f).astype(BF16)
            f = (r * r) * f + as_s[a, :, lanes]
    b_sums, c_sums = [], []
    for a in range(subs):
        b_sum, c_sum = sums[a]
        for h, lanes in enumerate(halves):
            b_sum = b_sum + dot(vx_s[block(a), lanes], states[h, a, 1], ((1,), (1,)))
            c_sum = c_sum + dot(ug_s[block(a), lanes], states[h, a, 0], ((1,), (1,)))
        b_sums.append(b_sum)
        c_sums.append(c_sum)
    part[:, 0] = jnp.concatenate(b_sums, axis=0).reshape(zs, rows, state)
    part[:, 1] = jnp.concatenate(c_sums, axis=0).reshape(zs, rows, state)
    scatters = [
        copy(part.at[(z + d) % zs], rpart.at[d - 1], r_send.at[d - 1], r_recv.at[d - 1], z_peer(d))
        for d in range(1, zs)
    ]
    for each in scatters:
        each.start()
    for a in range(subs):
        for h, lanes in enumerate(halves):
            out = od_s[block(a), lanes] + dot(c_all[block(a)], states[h, a, 0])
            out = u_s[block(a), lanes] * out
            out = out + gain_s[:, lanes] * x_ref[block(a), lanes].astype(F32)
            out_ref[block(a), lanes] = out.astype(BF16)
            grad = gd_s[block(a), lanes] + dot(b_all[block(a)], states[h, a, 1])
            grad = vs_s[block(a), lanes] * grad
            grad = grad + gain_s[:, lanes] * g_ref[block(a), lanes].astype(F32)
            ig_ref[block(a), lanes] = grad.astype(BF16)
    gb, gc = part[z, 0], part[z, 1]
    for d, each in enumerate(scatters):
        each.wait()
        gb = gb + rpart[d, 0]
        gc = gc + rpart[d, 1]
    gb_ref[...] = gb
    gc_ref[...] = gc


def local(x_in, b_in, c_in, decay_codes, decay_rate, skip_gain, out_grad):
    tokens, width = x_in.shape
    rows, state = b_in.shape
    heads = decay_codes.shape[0]
    subs = tokens // SUB
    half = width // 2
    chips = lax.axis_size("seq") // 2
    zs = lax.axis_size("head")
    vmem = pl.BlockSpec(memory_space=pltpu.VMEM)
    dma = pltpu.SemaphoreType.DMA
    return pl.pallas_call(
        functools.partial(kernel, chips, zs),
        out_shape=(
            jax.ShapeDtypeStruct((tokens, width), BF16),
            jax.ShapeDtypeStruct((tokens, width), BF16),
            jax.ShapeDtypeStruct((rows, state), F32),
            jax.ShapeDtypeStruct((rows, state), F32),
        ),
        in_specs=[vmem] * 7,
        out_specs=(vmem,) * 4,
        scratch_shapes=[
            pltpu.VMEM((tokens, width), F32),
            pltpu.VMEM((tokens, width), F32),
            pltpu.VMEM((tokens, width), BF16),
            pltpu.VMEM((tokens, width), BF16),
            pltpu.VMEM((tokens, width), F32),
            pltpu.VMEM((tokens, width), F32),
            pltpu.VMEM((subs, state, width), F32),
            pltpu.VMEM((subs, state, width), F32),
            pltpu.VMEM((1, width), F32),
            pltpu.VMEM((zs, 2, rows, state), BF16),
            pltpu.VMEM((2, 2, state, half), BF16),
            pltpu.VMEM((2, 1, half), F32),
            pltpu.VMEM((2, 2, state, half), BF16),
            pltpu.VMEM((2, 1, half), F32),
            pltpu.VMEM((2, state, half), BF16),
            pltpu.VMEM((1, half), F32),
            pltpu.VMEM((chips - 1, state, half), BF16),
            pltpu.VMEM((chips - 1, 1, half), F32),
            pltpu.VMEM((2, 2, state, half), BF16),
            pltpu.VMEM((2, 2, state, half), BF16),
            pltpu.VMEM((zs, 2, rows, state), F32),
            pltpu.VMEM((zs - 1, 2, rows, state), F32),
            dma((zs - 1,)), dma((zs - 1,)),
            dma((3,)), dma((3,)),
            dma((chips - 1,)), dma((chips - 1,)),
            dma((chips - 1,)), dma((chips - 1,)),
            dma((zs - 1,)), dma((zs - 1,)),
        ],
        compiler_params=pltpu.CompilerParams(
            collective_id=0, has_side_effects=True, vmem_limit_bytes=48 * 1024 * 1024
        ),
    )(
        x_in, b_in, c_in, decay_codes,
        decay_rate.reshape(1, heads), skip_gain.reshape(1, heads), out_grad,
    )


def solution(mesh):
    placed = (
        P("seq", "head"),
        P(("seq", "head"), None),
        P(("seq", "head"), None),
        P("head", "seq"),
        P("head"),
        P("head"),
        P("seq", "head"),
    )
    return jax.shard_map(
        local,
        mesh=mesh,
        in_specs=placed,
        out_specs=(
            P("seq", "head"),
            P("seq", "head"),
            P(("seq", "head"), None),
            P(("seq", "head"), None),
        ),
        check_vma=False,
    )
```

time: 192 us -> 47.3 us (0.25)
  waiting for transfers between devices: 73.4 us -> 0 us
  Pallas kernels: 0 us -> 37.8 us
  blocking collectives: 37 us -> 0 us
  matrix products: 32.2 us -> 0 us
  other arithmetic: 26.5 us -> 0 us
  between operations: 14 us -> 0.66 us
    all_gather x2 -> x0, waiting for transfers between devices: 60.5 us -> none  [carried_in(): everything = jax.tree.map(lambda part: lax.all_gather(part, axis), x)]
    pallas_call x0 -> x1, Pallas kernels: none -> 37.8 us  [local(): pl.pallas_call(functools.partial(kernel, chips, zs), out_shape=(jax.Shape...]
    all_gather x3 -> x0, blocking collectives: 37 us -> none  [the longest x1 14.9 us: local(): lax.all_gather(c_in, 'head', axis=0, tiled=True)]
    dot_general x12 -> x0, matrix products: 32.2 us -> none  [the longest x6 17.7 us: exact(): return jnp.einsum(form, *operands, precision=lax.Precision.HIGHEST)]
    select_n x16 -> x0, other arithmetic: 23.6 us -> none  [hop(): return jax.tree.map(lambda a, b: jnp.where(reached, a, b), new, before)]
    reduce_scatter x2 -> x0, waiting for transfers between devices: 12.8 us -> none  [the longest x1 12.8 us: local(): lax.psum_scatter(c_sum, 'head', scatter_dimension=0, tiled=True)]
    unnamed x21 -> x18, local copies, waits for them, and re-layouts: 4.35 us -> 8.47 us
  transfers between devices with their start and end apart: 4 -> 0, of which waited for: 3 -> 0; matrix products, arithmetic and copies ran while one was open for 31% -> 0% of each run, Pallas kernels for 0% -> 0%
where the time goes in v1:
time: 47.3 us; the launch traced here: 47 us
  Pallas kernels  37.8 us (80%)
  local copies, waits for them, and re-layouts  8.47 us (18%)
  between operations  0.66 us (1%)
    pallas_call x1, Pallas kernels, local(): pl.pallas_call(functools.partial(kernel, chips, zs), out_shape=(jax.Shape...  37.8 us
    unnamed x18, local copies, waits for them, and re-layouts  8.47 us

profile of v1, /device:TPU:0, one launch (start us, length us, event | category | flops | bytes accessed | tf_op | source)
XLA Modules:
  0.0 47.0 jit_solution(5751478729403343025)
XLA Ops:
  0.6 0.0 copy-start.5
  0.6 0.0 copy-start.6
  0.7 0.6 %copy-done.5 = f32[32]{0:T(128)S(1)} copy-done((f32[32]{0:T(128)S(1)}, f32[32]{0:T(128)}, u32[]{:S(2)}) %copy-start.5) | copy-done | bytes 152
  1.3 0.0 copy-done.6
  1.3 0.0 copy-start
  1.3 1.2 %copy-done = bf16[256,2048]{1,0:T(8,128)(2,1)S(1)} copy-done((bf16[256,2048]{1,0:T(8,128)(2,1)S(1)}, bf16[256,2048]{1,0:T(8,128)(2,1)}, u32[]{:S(2)}) %copy-start) | copy-done | bytes 1048600
  2.5 0.0 copy-start.1
  2.5 1.2 %copy-done.1 = bf16[256,2048]{1,0:T(8,128)(2,1)S(1)} copy-done((bf16[256,2048]{1,0:T(8,128)(2,1)S(1)}, bf16[256,2048]{1,0:T(8,128)(2,1)}, u32[]{:S(2)}) %copy-start.1) | copy-done | bytes 1048600
  3.8 0.0 copy-start.2
  3.8 0.8 %copy-done.2 = s32[32,256]{1,0:T(8,128)S(1)} copy-done((s32[32,256]{1,0:T(8,128)S(1)}, s32[32,256]{1,0:T(8,128)}, u32[]{:S(2)}) %copy-start.2) | copy-done | bytes 32792
  4.5 0.0 copy-start.3
  4.5 0.7 %copy-done.3 = bf16[64,128]{1,0:T(8,128)(2,1)S(1)} copy-done((bf16[64,128]{1,0:T(8,128)(2,1)S(1)}, bf16[64,128]{1,0:T(8,128)(2,1)}, u32[]{:S(2)}) %copy-start.3) | copy-done | bytes 16408
  5.2 0.0 copy-start.4
  5.2 0.7 %copy-done.4 = bf16[64,128]{1,0:T(8,128)(2,1)S(1)} copy-done((bf16[64,128]{1,0:T(8,128)(2,1)S(1)}, bf16[64,128]{1,0:T(8,128)(2,1)}, u32[]{:S(2)}) %copy-start.4) | copy-done | bytes 16408
  6.0 37.8 %shard_map.102 = (bf16[256,2048]{1,0:T(8,128)(2,1)S(1)}, bf16[256,2048]{1,0:T(8,128)(2,1)S(1)}, f32[64,128]{1,0:T(8,128)S(1)}, f32[64,128]{1,0:T(8,128)S(1)}) custom-call(bf16[256,2048]{1,0:T(8,128)(2,1)S(1)} %copy-done, bf16[64,128]{1,0:T(8,128)(2,1)S(1)} %copy-done.3, bf16[64,128]{1,0:T(8,128)(2,1)S(1)} %copy-done.4, s32[32,256]{1,0:T(8,128)S(1)} %copy-done.2, ...), custom_call_target="tpu_custom_call" | custom-call | tf_op jit(solution)/shard_map/pallas_call | solution.py:258
  43.8 1.0 %copy.15 = bf16[256,2048]{1,0:T(8,128)(2,1)} copy(bf16[256,2048]{1,0:T(8,128)(2,1)S(1)} %get-tuple-element.8) | data formatting | bytes 2097152
  44.8 1.0 %copy.16 = bf16[256,2048]{1,0:T(8,128)(2,1)} copy(bf16[256,2048]{1,0:T(8,128)(2,1)S(1)} %get-tuple-element.9) | data formatting | bytes 2097152
  45.7 0.6 %copy.17 = f32[64,128]{1,0:T(8,128)} copy(f32[64,128]{1,0:T(8,128)S(1)} %get-tuple-element.10) | data formatting | bytes 65536
  46.3 0.6 %copy.18 = f32[64,128]{1,0:T(8,128)} copy(f32[64,128]{1,0:T(8,128)S(1)} %get-tuple-element.11) | data formatting | bytes 65536
Async XLA Ops:
  0.6 0.7 %copy-start.5 = (f32[32]{0:T(128)S(1)}, f32[32]{0:T(128)}, u32[]{:S(2)}) copy-start(f32[32]{0:T(128)} %param.11) | copy-start | bytes 388
  0.6 0.7 %copy-start.6 = (f32[32]{0:T(128)S(1)}, f32[32]{0:T(128)}, u32[]{:S(2)}) copy-start(f32[32]{0:T(128)} %param.12) | copy-start | bytes 388
  1.3 1.2 %copy-start = (bf16[256,2048]{1,0:T(8,128)(2,1)S(1)}, bf16[256,2048]{1,0:T(8,128)(2,1)}, u32[]{:S(2)}) copy-start(bf16[256,2048]{1,0:T(8,128)(2,1)} %x_ref.1) | copy-start | bytes 3145732
  2.5 1.2 %copy-start.1 = (bf16[256,2048]{1,0:T(8,128)(2,1)S(1)}, bf16[256,2048]{1,0:T(8,128)(2,1)}, u32[]{:S(2)}) copy-start(bf16[256,2048]{1,0:T(8,128)(2,1)} %g_ref.1) | copy-start | bytes 3145732
  3.8 0.8 %copy-start.2 = (s32[32,256]{1,0:T(8,128)S(1)}, s32[32,256]{1,0:T(8,128)}, u32[]{:S(2)}) copy-start(s32[32,256]{1,0:T(8,128)} %codes_ref.1) | copy-start | bytes 98308
  4.5 0.7 %copy-start.3 = (bf16[64,128]{1,0:T(8,128)(2,1)S(1)}, bf16[64,128]{1,0:T(8,128)(2,1)}, u32[]{:S(2)}) copy-start(bf16[64,128]{1,0:T(8,128)(2,1)} %b_ref.1) | copy-start | bytes 49156
  5.2 0.7 %copy-start.4 = (bf16[64,128]{1,0:T(8,128)(2,1)S(1)}, bf16[64,128]{1,0:T(8,128)(2,1)}, u32[]{:S(2)}) copy-start(bf16[64,128]{1,0:T(8,128)(2,1)} %c_ref.1) | copy-start | bytes 49156

commit v2 on v1

v2 whole, which is shorter than its diff:
```python
import functools

import jax
import jax.numpy as jnp
from jax import lax
from jax.experimental import pallas as pl
from jax.experimental.pallas import tpu as pltpu
from jax.sharding import PartitionSpec as P

SUB = 128
MESH = pl.DeviceIdType.MESH
F32 = jnp.float32
BF16 = jnp.bfloat16


def dot(a, b, dims=((1,), (0,))):
    return lax.dot_general(a, b, (dims, ((), ())), preferred_element_type=F32)


def split3(a):
    hi = a.astype(BF16).astype(F32)
    mid = (a - hi).astype(BF16).astype(F32)
    low = a - hi - mid
    return jnp.concatenate([hi, mid, low], axis=0)


def split_dot(a, b, dims=((1,), (0,))):
    hi = a.astype(BF16)
    low = (a - hi.astype(F32)).astype(BF16)
    return dot(hi, b, dims) + dot(low, b, dims)


def kernel(
    chips, zs, parts,
    x_hbm, b_hbm, c_hbm, codes_hbm, rate_hbm, gain_hbm, g_hbm,
    out_hbm, ig_hbm, gb_ref, gc_ref,
    out_ref, ig_ref, x_ref, g_ref, codes_ref, rate_ref, gain_ref,
    u_s, vs_s, ug_s, vx_s, od_s, gd_s, ps_s, as_s, gain_s, spread_s,
    bc, pa, dd, pc, dc, qb, qt, rq, rt, tmp, ef, part, rpart,
    l_sem, g_send, g_recv, d_send, d_recv, s_send, s_recv, e_send, e_recv,
    q_send, q_recv, t_send, t_recv, r_send, r_recv, o_sem,
):
    tokens, width = x_ref.shape
    heads = codes_ref.shape[0]
    dim = width // heads
    rows, state = b_hbm.shape
    subs = tokens // SUB
    half = width // 2
    size = half // parts
    seq = lax.axis_index("seq")
    z = lax.axis_index("head")
    chip = seq // 2
    core = seq % 2
    other = 1 - core
    sib = {"seq": chip * 2 + other, "head": z}

    def z_peer(d):
        return {"seq": seq, "head": (z + d) % zs}

    def chip_peer(d):
        return {"seq": ((chip + d) % chips) * 2 + core, "head": z}

    def copy(src, dst, send, recv, to):
        return pltpu.make_async_remote_copy(
            src_ref=src, dst_ref=dst, send_sem=send, recv_sem=recv,
            device_id=to, device_id_type=MESH,
        )

    loads = [
        pltpu.make_async_copy(src, dst, l_sem.at[i])
        for i, (src, dst) in enumerate([
            (codes_hbm, codes_ref), (rate_hbm, rate_ref), (gain_hbm, gain_ref),
            (b_hbm, bc.at[z, 0]), (c_hbm, bc.at[z, 1]), (g_hbm, g_ref), (x_hbm, x_ref),
        ])
    ]
    for each in loads:
        each.start()
    barrier = pltpu.get_barrier_semaphore()
    for d in range(1, zs):
        pl.semaphore_signal(barrier, inc=1, device_id=z_peer(d), device_id_type=MESH)
    for d in range(1, chips):
        pl.semaphore_signal(barrier, inc=1, device_id=chip_peer(d), device_id_type=MESH)
    pl.semaphore_signal(barrier, inc=1, device_id=sib, device_id_type=MESH)
    for each in loads[:5]:
        each.wait()
    pl.semaphore_wait(barrier, zs + chips - 1)
    gathers = [
        copy(bc.at[z], bc.at[z], g_send.at[d - 1], g_recv.at[d - 1], z_peer(d))
        for d in range(1, zs)
    ]
    for each in gathers:
        each.start()

    eye = lax.broadcasted_iota(jnp.int32, (heads, heads), 0) == lax.broadcasted_iota(
        jnp.int32, (heads, heads), 1
    )
    rate = jnp.sum(jnp.where(eye, rate_ref[...], 0.0), axis=1, keepdims=True)
    gain = jnp.sum(jnp.where(eye, gain_ref[...], 0.0), axis=1, keepdims=True)
    codes = codes_ref[...]
    step = 0.5 + (codes & 1023).astype(F32) * (1.0 / 1024.0)
    log_decay = -rate * step - 0.1 * (codes >> 10).astype(F32)
    at_u = lax.broadcasted_iota(jnp.int32, (tokens, tokens), 0)
    at_t = lax.broadcasted_iota(jnp.int32, (tokens, tokens), 1)
    centred = jnp.where(
        at_u // SUB == at_t // SUB, jnp.where(at_u <= at_t, 0.5, -0.5), 0.0
    ).astype(BF16)
    logs = dot(split3(log_decay).astype(BF16), centred)
    logs = logs[:heads] + logs[heads : 2 * heads] + logs[2 * heads :]
    u3 = split3(jnp.exp(logs)).T.astype(BF16)
    v3 = split3(jnp.exp(-logs) * step).T.astype(BF16)
    lane = lax.broadcasted_iota(jnp.int32, (heads, width), 1)
    first = lax.broadcasted_iota(jnp.int32, (heads, width), 0) * dim
    own = (lane >= first) & (lane < first + dim)
    gain_s[...] = jnp.sum(jnp.where(own, gain, 0.0), axis=0, keepdims=True)
    total = jnp.exp(jnp.sum(log_decay, axis=1, keepdims=True))
    total = jnp.sum(jnp.where(own, total, 0.0), axis=0, keepdims=True)
    dd[0] = total[:, :half]
    dd[1] = total[:, half:]
    spread_s[...] = jnp.concatenate([own.astype(F32)] * 3, axis=0).astype(BF16)
    to_sib = copy(dd.at[other], dc.at[core], d_send.at[0], d_recv.at[0], sib)
    to_sib.start()
    dc[core] = dd[core]
    for each in loads[5:]:
        each.wait()

    def block(a):
        return slice(a * SUB, (a + 1) * SUB)

    def chunk(h, k):
        return slice(h * half + k * size, h * half + (k + 1) * size)

    def root(a, lanes):
        return u_s[(a + 1) * SUB - 1 : (a + 1) * SUB, lanes]

    def factors(k):
        for h in range(2):
            lanes = chunk(h, k)
            u = dot(u3, spread_s[:, lanes])
            vs = dot(v3, spread_s[:, lanes])
            u_s[:, lanes] = u
            vs_s[:, lanes] = vs
            ug_s[:, lanes] = (u * g_ref[:, lanes].astype(F32)).astype(BF16)
            vx_s[:, lanes] = (vs * x_ref[:, lanes].astype(F32)).astype(BF16)

    early = (parts + 1) // 2
    for k in range(early):
        factors(k)
    for each in gathers:
        each.wait()
    b_all = bc[:, 0].reshape(tokens, state)
    c_all = bc[:, 1].reshape(tokens, state)
    b_flip = b_all.astype(F32).T.astype(BF16)
    c_flip = c_all.astype(F32).T.astype(BF16)

    sib_copies = [
        copy(pa.at[other, k], pc.at[core, k], s_send.at[k], s_recv.at[k], sib)
        for k in range(parts)
    ]

    def summarize(k):
        for h in range(2):
            lanes = chunk(h, k)
            total = None
            for a in range(subs):
                r = root(a, lanes)
                ps = r * dot(b_flip[:, block(a)], vx_s[block(a), lanes])
                ad = r * dot(c_flip[:, block(a)], ug_s[block(a), lanes])
                ps_s[a, :, lanes] = ps
                as_s[a, :, lanes] = ad
                if a == 0:
                    p_dev, a_dev, total = ps, ad, r * r
                else:
                    p_dev = (r * r) * p_dev + ps
                    a_dev = a_dev + total * ad
                    total = total * (r * r)
            pa[h, k, 0] = p_dev
            pa[h, k, 1] = a_dev
        sib_copies[k].start()
        pc[core, k] = pa[core, k]

    to_chips = {}

    def combine(k):
        here = slice(k * size, (k + 1) * size)
        if k == 0:
            to_sib.wait()
            qt[...] = dc[0] * dc[1]
            for d in range(1, chips):
                each = copy(qt, rt.at[d - 1], t_send.at[d - 1], t_recv.at[d - 1], chip_peer(d))
                each.start()
                to_chips[d] = each
        sib_copies[k].wait()
        qb[k, 0] = (dc[1, :, here] * pc[0, k, 0] + pc[1, k, 0]).astype(BF16)
        qb[k, 1] = (pc[0, k, 1] + dc[0, :, here] * pc[1, k, 1]).astype(BF16)
        for d in range(1, chips):
            each = copy(
                qb.at[k, (chip + d) // chips], rq.at[k, d - 1],
                q_send.at[k, d - 1], q_recv.at[k, d - 1], chip_peer(d),
            )
            each.start()
            to_chips[k, d] = each

    summarize(0)
    for k in range(1, parts):
        if k >= early:
            factors(k)
        summarize(k)
        combine(k - 1)
    combine(parts - 1)

    at_r = lax.broadcasted_iota(jnp.int32, (SUB, SUB), 0)
    at_c = lax.broadcasted_iota(jnp.int32, (SUB, SUB), 1)
    b_sums, c_sums = [], []
    for a in range(subs):
        b_a, c_a = b_all[block(a)], c_all[block(a)]
        scores = jnp.where(at_r >= at_c, dot(c_a, b_a, ((1,), (1,))), 0.0).astype(BF16)
        flipped = jnp.where(at_r <= at_c, dot(b_a, c_a, ((1,), (1,))), 0.0).astype(BF16)
        od_s[block(a)] = dot(scores, vx_s[block(a)])
        gd_s[block(a)] = dot(flipped, ug_s[block(a)])
        paired = dot(ug_s[block(a)], vx_s[block(a)], ((1,), (1,)))
        paired = jnp.where(at_r >= at_c, paired, 0.0)
        b_sums.append(split_dot(paired.T, c_a))
        c_sums.append(split_dot(paired, b_a))

    back = [
        copy(tmp.at[other, k], ef.at[core, k], e_send.at[k], e_recv.at[k], sib)
        for k in range(parts)
    ]

    def enter(k):
        here = slice(k * size, (k + 1) * size)
        for d in range(1, chips):
            if k == 0:
                to_chips[d].wait()
            to_chips[k, d].wait()
        e_in = jnp.zeros((state, size), F32)
        f_in = jnp.zeros((state, size), F32)
        reach = jnp.ones((1, size), F32)
        for d in range(1, chips):
            e_in = e_in + jnp.where(chip >= d, reach, 0.0) * rq[k, d - 1].astype(F32)
            reach = reach * rt[d - 1, :, here]
        reach = jnp.ones((1, size), F32)
        for d in range(chips - 1, 0, -1):
            f_in = f_in + jnp.where(chip < d, reach, 0.0) * rq[k, d - 1].astype(F32)
            reach = reach * rt[d - 1, :, here]
        tmp[0, k, 0] = e_in
        tmp[1, k, 0] = dc[0, :, here] * e_in + pc[0, k, 0]
        tmp[1, k, 1] = f_in
        tmp[0, k, 1] = dc[1, :, here] * f_in + pc[1, k, 1]
        back[k].start()
        ef[core, k] = tmp[core, k]

    def states(k):
        back[k].wait()
        es = {}
        for h in range(2):
            lanes = chunk(h, k)
            e, f = ef[h, k, 0], ef[h, k, 1]
            for a in range(subs):
                r = root(a, lanes)
                es[h, a, 0] = (r * e).astype(BF16)
                if a < subs - 1:
                    e = (r * r) * e + ps_s[a, :, lanes]
            for a in range(subs - 1, -1, -1):
                r = root(a, lanes)
                es[h, a, 1] = (r * f).astype(BF16)
                if a > 0:
                    f = (r * r) * f + as_s[a, :, lanes]
            for a in range(subs):
                b_sums[a] += dot(vx_s[block(a), lanes], es[h, a, 1], ((1,), (1,)))
                c_sums[a] += dot(ug_s[block(a), lanes], es[h, a, 0], ((1,), (1,)))
        return es

    stores = []

    def outputs(k, es):
        for h in range(2):
            lanes = chunk(h, k)
            for a in range(subs):
                out = od_s[block(a), lanes] + dot(c_all[block(a)], es[h, a, 0])
                out = u_s[block(a), lanes] * out
                out = out + gain_s[:, lanes] * x_ref[block(a), lanes].astype(F32)
                out_ref[block(a), lanes] = out.astype(BF16)
                grad = gd_s[block(a), lanes] + dot(b_all[block(a)], es[h, a, 1])
                grad = vs_s[block(a), lanes] * grad
                grad = grad + gain_s[:, lanes] * g_ref[block(a), lanes].astype(F32)
                ig_ref[block(a), lanes] = grad.astype(BF16)
            for i, (src, dst) in enumerate([(out_ref, out_hbm), (ig_ref, ig_hbm)]):
                each = pltpu.make_async_copy(src.at[:, lanes], dst.at[:, lanes], o_sem.at[k, h, i])
                each.start()
                stores.append(each)

    enter(0)
    for k in range(1, parts):
        enter(k)
        outputs(k - 1, states(k - 1))
    last = states(parts - 1)
    part[:, 0] = jnp.concatenate(b_sums, axis=0).reshape(zs, rows, state)
    part[:, 1] = jnp.concatenate(c_sums, axis=0).reshape(zs, rows, state)
    scatters = [
        copy(part.at[(z + d) % zs], rpart.at[d - 1], r_send.at[d - 1], r_recv.at[d - 1], z_peer(d))
        for d in range(1, zs)
    ]
    for each in scatters:
        each.start()
    outputs(parts - 1, last)
    gb, gc = part[z, 0], part[z, 1]
    for d, each in enumerate(scatters):
        each.wait()
        gb = gb + rpart[d, 0]
        gc = gc + rpart[d, 1]
    gb_ref[...] = gb
    gc_ref[...] = gc
    for each in stores:
        each.wait()


def local(x_in, b_in, c_in, decay_codes, decay_rate, skip_gain, out_grad):
    tokens, width = x_in.shape
    rows, state = b_in.shape
    heads = decay_codes.shape[0]
    subs = tokens // SUB
    half = width // 2
    parts = max(1, min(4, half // 128))
    size = half // parts
    chips = lax.axis_size("seq") // 2
    zs = lax.axis_size("head")
    vmem = pl.BlockSpec(memory_space=pltpu.VMEM)
    hbm = pl.BlockSpec(memory_space=pltpu.MemorySpace.HBM)
    dma = pltpu.SemaphoreType.DMA
    return pl.pallas_call(
        functools.partial(kernel, chips, zs, parts),
        out_shape=(
            jax.ShapeDtypeStruct((tokens, width), BF16),
            jax.ShapeDtypeStruct((tokens, width), BF16),
            jax.ShapeDtypeStruct((rows, state), F32),
            jax.ShapeDtypeStruct((rows, state), F32),
        ),
        in_specs=[hbm] * 7,
        out_specs=(hbm, hbm, vmem, vmem),
        scratch_shapes=[
            pltpu.VMEM((tokens, width), BF16),
            pltpu.VMEM((tokens, width), BF16),
            pltpu.VMEM((tokens, width), BF16),
            pltpu.VMEM((tokens, width), BF16),
            pltpu.VMEM(decay_codes.shape, jnp.int32),
            pltpu.VMEM((1, heads), F32),
            pltpu.VMEM((1, heads), F32),
            pltpu.VMEM((tokens, width), F32),
            pltpu.VMEM((tokens, width), F32),
            pltpu.VMEM((tokens, width), BF16),
            pltpu.VMEM((tokens, width), BF16),
            pltpu.VMEM((tokens, width), F32),
            pltpu.VMEM((tokens, width), F32),
            pltpu.VMEM((subs, state, width), F32),
            pltpu.VMEM((subs, state, width), F32),
            pltpu.VMEM((1, width), F32),
            pltpu.VMEM((3 * heads, width), BF16),
            pltpu.VMEM((zs, 2, rows, state), BF16),
            pltpu.VMEM((2, parts, 2, state, size), F32),
            pltpu.VMEM((2, 1, half), F32),
            pltpu.VMEM((2, parts, 2, state, size), F32),
            pltpu.VMEM((2, 1, half), F32),
            pltpu.VMEM((parts, 2, state, size), BF16),
            pltpu.VMEM((1, half), F32),
            pltpu.VMEM((parts, chips - 1, state, size), BF16),
            pltpu.VMEM((chips - 1, 1, half), F32),
            pltpu.VMEM((2, parts, 2, state, size), F32),
            pltpu.VMEM((2, parts, 2, state, size), F32),
            pltpu.VMEM((zs, 2, rows, state), F32),
            pltpu.VMEM((zs - 1, 2, rows, state), F32),
            dma((7,)),
            dma((zs - 1,)), dma((zs - 1,)),
            dma((1,)), dma((1,)),
            dma((parts,)), dma((parts,)),
            dma((parts,)), dma((parts,)),
            dma((parts, chips - 1)), dma((parts, chips - 1)),
            dma((chips - 1,)), dma((chips - 1,)),
            dma((zs - 1,)), dma((zs - 1,)),
            dma((parts, 2, 2)),
        ],
        compiler_params=pltpu.CompilerParams(
            collective_id=0, has_side_effects=True, vmem_limit_bytes=61 * 1024 * 1024
        ),
    )(
        x_in, b_in, c_in, decay_codes,
        decay_rate.reshape(1, heads), skip_gain.reshape(1, heads), out_grad,
    )


def solution(mesh):
    placed = (
        P("seq", "head"),
        P(("seq", "head"), None),
        P(("seq", "head"), None),
        P("head", "seq"),
        P("head"),
        P("head"),
        P("seq", "head"),
    )
    return jax.shard_map(
        local,
        mesh=mesh,
        in_specs=placed,
        out_specs=(
            P("seq", "head"),
            P("seq", "head"),
            P(("seq", "head"), None),
            P(("seq", "head"), None),
        ),
        check_vma=False,
    )
```

time: 47.3 us -> 40.3 us (0.85)
  local copies, waits for them, and re-layouts: 8.47 us -> 4.75 us
  Pallas kernels: 37.8 us -> 34.7 us
    unnamed x18 -> x10, local copies, waits for them, and re-layouts: 8.47 us -> 4.75 us
    pallas_call x1, Pallas kernels: 37.8 us -> 34.7 us  [local(): pl.pallas_call(functools.partial(kernel, chips, zs, parts), out_shape=(ja...]
where the time goes in v2:
time: 40.3 us; the launch traced here: 40.1 us
  Pallas kernels  34.7 us (86%)
  local copies, waits for them, and re-layouts  4.75 us (12%)
  between operations  0.65 us (2%)
    pallas_call x1, Pallas kernels, local(): pl.pallas_call(functools.partial(kernel, chips, zs, parts), out_shape=(ja...  34.7 us
    unnamed x10, local copies, waits for them, and re-layouts  4.75 us

profile of v2, /device:TPU:0, one launch (start us, length us, event | category | flops | bytes accessed | tf_op | source)
XLA Modules:
  0.0 40.1 jit_solution(8121587436872663093)
XLA Ops:
  0.6 34.7 %shard_map.102 = (bf16[256,2048]{1,0:T(8,128)(2,1)}, bf16[256,2048]{1,0:T(8,128)(2,1)}, f32[64,128]{1,0:T(8,128)}, f32[64,128]{1,0:T(8,128)}) custom-call(bf16[256,2048]{1,0:T(8,128)(2,1)} %x_hbm.1, bf16[64,128]{1,0:T(8,128)(2,1)} %b_hbm.1, bf16[64,128]{1,0:T(8,128)(2,1)} %c_hbm.1, s32[32,256]{1,0:T(8,128)} %codes_hbm.1, f32[1,32]{1,0:T(1,128)} %bitcast.2, ...), custom_call_target="tpu_custom_call" | custom-call | tf_op jit(solution)/shard_map/pallas_call | solution.py:331
  35.3 0.0 copy-start
  35.3 2.4 %copy.15 = bf16[256,2048]{1,0:T(8,128)(2,1)} copy(bf16[256,2048]{1,0:T(8,128)(2,1)} %get-tuple-element.8) | data formatting | bytes 2097152
  37.7 0.0 copy-done
  37.7 0.0 copy-start.2
  37.7 1.0 %copy.16 = bf16[256,2048]{1,0:T(8,128)(2,1)} copy(bf16[256,2048]{1,0:T(8,128)(2,1)S(1)} %copy-done) | data formatting | bytes 2097152
  38.7 0.0 copy-done.2
  38.7 0.0 copy-start.1
  38.7 0.6 %copy.17 = f32[64,128]{1,0:T(8,128)} copy(f32[64,128]{1,0:T(8,128)S(1)} %copy-done.2) | data formatting | bytes 65536
  39.3 0.2 copy-done.1
  39.5 0.6 %copy.18 = f32[64,128]{1,0:T(8,128)} copy(f32[64,128]{1,0:T(8,128)S(1)} %copy-done.1) | data formatting | bytes 65536
Async XLA Ops:
  35.3 2.4 %copy-start = (bf16[256,2048]{1,0:T(8,128)(2,1)S(1)}, bf16[256,2048]{1,0:T(8,128)(2,1)}, u32[]{:S(2)}) copy-start(bf16[256,2048]{1,0:T(8,128)(2,1)} %get-tuple-element.9) | copy-start | bytes 3145732
  37.7 1.0 %copy-start.2 = (f32[64,128]{1,0:T(8,128)S(1)}, f32[64,128]{1,0:T(8,128)}, u32[]{:S(2)}) copy-start(f32[64,128]{1,0:T(8,128)} %get-tuple-element.10) | copy-start | bytes 98308
  38.7 0.8 %copy-start.1 = (f32[64,128]{1,0:T(8,128)S(1)}, f32[64,128]{1,0:T(8,128)}, u32[]{:S(2)}) copy-start(f32[64,128]{1,0:T(8,128)} %get-tuple-element.11) | copy-start | bytes 98308

commit v3 on v2

--- a/solution.py
+++ b/solution.py
@@ -36,9 +36,9 @@
     out_hbm, ig_hbm, gb_ref, gc_ref,
     out_ref, ig_ref, x_ref, g_ref, codes_ref, rate_ref, gain_ref,
     u_s, vs_s, ug_s, vx_s, od_s, gd_s, ps_s, as_s, gain_s, spread_s,
-    bc, pa, dd, pc, dc, qb, qt, rq, rt, tmp, ef, part, rpart,
+    bc, pa, dd, pc, dc, qb, qt, rq, rt, tmp, ef, part, rpart, late, lpart, rlate,
     l_sem, g_send, g_recv, d_send, d_recv, s_send, s_recv, e_send, e_recv,
-    q_send, q_recv, t_send, t_recv, r_send, r_recv, o_sem,
+    q_send, q_recv, t_send, t_recv, r_send, r_recv, w_send, w_recv, o_sem,
 ):
     tokens, width = x_ref.shape
     heads = codes_ref.shape[0]
@@ -112,10 +112,15 @@
     first = lax.broadcasted_iota(jnp.int32, (heads, width), 0) * dim
     own = (lane >= first) & (lane < first + dim)
     gain_s[...] = jnp.sum(jnp.where(own, gain, 0.0), axis=0, keepdims=True)
-    total = jnp.exp(jnp.sum(log_decay, axis=1, keepdims=True))
-    total = jnp.sum(jnp.where(own, total, 0.0), axis=0, keepdims=True)
-    dd[0] = total[:, :half]
-    dd[1] = total[:, half:]
+    ends = [
+        jnp.exp(jnp.sum(log_decay, axis=1, keepdims=True)),
+        jnp.exp(logs[:, SUB - 1 : SUB]),
+        jnp.exp(logs[:, tokens - 1 :]),
+    ]
+    for i, end in enumerate(ends):
+        end = jnp.sum(jnp.where(own, end, 0.0), axis=0, keepdims=True)
+        dd[0, i] = end[:, :half]
+        dd[1, i] = end[:, half:]
     spread_s[...] = jnp.concatenate([own.astype(F32)] * 3, axis=0).astype(BF16)
     to_sib = copy(dd.at[other], dc.at[core], d_send.at[0], d_recv.at[0], sib)
     to_sib.start()
@@ -142,7 +147,7 @@
             ug_s[:, lanes] = (u * g_ref[:, lanes].astype(F32)).astype(BF16)
             vx_s[:, lanes] = (vs * x_ref[:, lanes].astype(F32)).astype(BF16)
 
-    early = (parts + 1) // 2
+    early = parts
     for k in range(early):
         factors(k)
     for each in gathers:
@@ -184,14 +189,14 @@
         here = slice(k * size, (k + 1) * size)
         if k == 0:
             to_sib.wait()
-            qt[...] = dc[0] * dc[1]
+            qt[...] = dc[0, 0] * dc[1, 0]
             for d in range(1, chips):
                 each = copy(qt, rt.at[d - 1], t_send.at[d - 1], t_recv.at[d - 1], chip_peer(d))
                 each.start()
                 to_chips[d] = each
         sib_copies[k].wait()
-        qb[k, 0] = (dc[1, :, here] * pc[0, k, 0] + pc[1, k, 0]).astype(BF16)
-        qb[k, 1] = (pc[0, k, 1] + dc[0, :, here] * pc[1, k, 1]).astype(BF16)
+        qb[k, 0] = (dc[1, 0, :, here] * pc[0, k, 0] + pc[1, k, 0]).astype(BF16)
+        qb[k, 1] = (pc[0, k, 1] + dc[0, 0, :, here] * pc[1, k, 1]).astype(BF16)
         for d in range(1, chips):
             each = copy(
                 qb.at[k, (chip + d) // chips], rq.at[k, d - 1],
@@ -243,10 +248,12 @@
         for d in range(chips - 1, 0, -1):
             f_in = f_in + jnp.where(chip < d, reach, 0.0) * rq[k, d - 1].astype(F32)
             reach = reach * rt[d - 1, :, here]
-        tmp[0, k, 0] = e_in
-        tmp[1, k, 0] = dc[0, :, here] * e_in + pc[0, k, 0]
-        tmp[1, k, 1] = f_in
-        tmp[0, k, 1] = dc[1, :, here] * f_in + pc[1, k, 1]
+        e_out = dc[0, 0, :, here] * e_in + pc[0, k, 0]
+        f_out = dc[1, 0, :, here] * f_in + pc[1, k, 1]
+        tmp[0, k, 0] = (dc[0, 1, :, here] * e_in).astype(BF16)
+        tmp[1, k, 0] = (dc[1, 1, :, here] * e_out).astype(BF16)
+        tmp[1, k, 1] = (dc[1, 2, :, here] * f_in).astype(BF16)
+        tmp[0, k, 1] = (dc[0, 2, :, here] * f_out).astype(BF16)
         back[k].start()
         ef[core, k] = tmp[core, k]
 
@@ -255,17 +262,18 @@
         es = {}
         for h in range(2):
             lanes = chunk(h, k)
-            e, f = ef[h, k, 0], ef[h, k, 1]
-            for a in range(subs):
+            es[h, 0, 0] = ef[h, k, 0]
+            es[h, subs - 1, 1] = ef[h, k, 1]
+            e = ef[h, k, 0].astype(F32)
+            for a in range(1, subs):
                 r = root(a, lanes)
-                es[h, a, 0] = (r * e).astype(BF16)
-                if a < subs - 1:
-                    e = (r * r) * e + ps_s[a, :, lanes]
-            for a in range(subs - 1, -1, -1):
+                e = r * (root(a - 1, lanes) * e + ps_s[a - 1, :, lanes])
+                es[h, a, 0] = e.astype(BF16)
+            f = ef[h, k, 1].astype(F32)
+            for a in range(subs - 2, -1, -1):
                 r = root(a, lanes)
-                es[h, a, 1] = (r * f).astype(BF16)
-                if a > 0:
-                    f = (r * r) * f + as_s[a, :, lanes]
+                f = r * (root(a + 1, lanes) * f + as_s[a + 1, :, lanes])
+                es[h, a, 1] = f.astype(BF16)
             for a in range(subs):
                 b_sums[a] += dot(vx_s[block(a), lanes], es[h, a, 1], ((1,), (1,)))
                 c_sums[a] += dot(ug_s[block(a), lanes], es[h, a, 0], ((1,), (1,)))
@@ -290,28 +298,67 @@
                 each.start()
                 stores.append(each)
 
+    def scatter(src, dst, send, recv):
+        copies = [
+            copy(src.at[(z + d) % zs], dst.at[d - 1], send.at[d - 1], recv.at[d - 1], z_peer(d))
+            for d in range(1, zs)
+        ]
+        for each in copies:
+            each.start()
+        return copies
+
+    def scatter_early():
+        part[:, 0] = jnp.concatenate(b_sums, axis=0).reshape(zs, rows, state)
+        part[:, 1] = jnp.concatenate(c_sums, axis=0).reshape(zs, rows, state)
+        for a in range(subs):
+            b_sums[a] = jnp.zeros((SUB, state), F32)
+            c_sums[a] = jnp.zeros((SUB, state), F32)
+        return scatter(part, rpart, r_send, r_recv)
+
+    if parts < 3:
+        sent = scatter_early()
     enter(0)
     for k in range(1, parts):
         enter(k)
-        outputs(k - 1, states(k - 1))
-    last = states(parts - 1)
-    part[:, 0] = jnp.concatenate(b_sums, axis=0).reshape(zs, rows, state)
-    part[:, 1] = jnp.concatenate(c_sums, axis=0).reshape(zs, rows, state)
-    scatters = [
-        copy(part.at[(z + d) % zs], rpart.at[d - 1], r_send.at[d - 1], r_recv.at[d - 1], z_peer(d))
-        for d in range(1, zs)
-    ]
-    for each in scatters:
-        each.start()
-    outputs(parts - 1, last)
-    gb, gc = part[z, 0], part[z, 1]
-    for d, each in enumerate(scatters):
-        each.wait()
+        es = states(k - 1)
+        if k == parts - 2:
+            sent = scatter_early()
+        outputs(k - 1, es)
+    es = states(parts - 1)
+    late[:, 0] = jnp.concatenate(b_sums, axis=0).reshape(zs, rows, state)
+    late[:, 1] = jnp.concatenate(c_sums, axis=0).reshape(zs, rows, state)
+    lpart[...] = late[...].astype(BF16)
+    sent_late = scatter(lpart, rlate, w_send, w_recv)
+    outputs(parts - 1, es)
+    gb = part[z, 0] + late[z, 0]
+    gc = part[z, 1] + late[z, 1]
+    for d in range(zs - 1):
+        sent[d].wait()
         gb = gb + rpart[d, 0]
         gc = gc + rpart[d, 1]
+    for d in range(zs - 1):
+        sent_late[d].wait()
+        gb = gb + rlate[d, 0].astype(F32)
+        gc = gc + rlate[d, 1].astype(F32)
     gb_ref[...] = gb
     gc_ref[...] = gc
     for each in stores:
+        each.wait()
+
+
+def hand_over(*refs):
+    count = (len(refs) - 1) // 2
+    sems = refs[-1]
+    copies = []
+    for i in range(count):
+        src, dst = refs[i], refs[count + i]
+        rows = src.shape[0] // 4
+        for j in range(4):
+            here = pl.ds(j * rows, rows)
+            copies.append(pltpu.make_async_copy(src.at[here], dst.at[here], sems.at[i, j]))
+    for each in copies:
+        each.start()
+    for each in copies:
         each.wait()
 
 
@@ -328,7 +375,7 @@
     vmem = pl.BlockSpec(memory_space=pltpu.VMEM)
     hbm = pl.BlockSpec(memory_space=pltpu.MemorySpace.HBM)
     dma = pltpu.SemaphoreType.DMA
-    return pl.pallas_call(
+    results = pl.pallas_call(
         functools.partial(kernel, chips, zs, parts),
         out_shape=(
             jax.ShapeDtypeStruct((tokens, width), BF16),
@@ -358,17 +405,20 @@
             pltpu.VMEM((3 * heads, width), BF16),
             pltpu.VMEM((zs, 2, rows, state), BF16),
             pltpu.VMEM((2, parts, 2, state, size), F32),
-            pltpu.VMEM((2, 1, half), F32),
+            pltpu.VMEM((2, 3, 1, half), F32),
             pltpu.VMEM((2, parts, 2, state, size), F32),
-            pltpu.VMEM((2, 1, half), F32),
+            pltpu.VMEM((2, 3, 1, half), F32),
             pltpu.VMEM((parts, 2, state, size), BF16),
             pltpu.VMEM((1, half), F32),
             pltpu.VMEM((parts, chips - 1, state, size), BF16),
             pltpu.VMEM((chips - 1, 1, half), F32),
-            pltpu.VMEM((2, parts, 2, state, size), F32),
-            pltpu.VMEM((2, parts, 2, state, size), F32),
+            pltpu.VMEM((2, parts, 2, state, size), BF16),
+            pltpu.VMEM((2, parts, 2, state, size), BF16),
             pltpu.VMEM((zs, 2, rows, state), F32),
             pltpu.VMEM((zs - 1, 2, rows, state), F32),
+            pltpu.VMEM((zs, 2, rows, state), F32),
+            pltpu.VMEM((zs, 2, rows, state), BF16),
+            pltpu.VMEM((zs - 1, 2, rows, state), BF16),
             dma((7,)),
             dma((zs - 1,)), dma((zs - 1,)),
             dma((1,)), dma((1,)),
@@ -376,6 +426,7 @@
             dma((parts,)), dma((parts,)),
             dma((parts, chips - 1)), dma((parts, chips - 1)),
             dma((chips - 1,)), dma((chips - 1,)),
+            dma((zs - 1,)), dma((zs - 1,)),
             dma((zs - 1,)), dma((zs - 1,)),
             dma((parts, 2, 2)),
         ],
@@ -386,6 +437,14 @@
         x_in, b_in, c_in, decay_codes,
         decay_rate.reshape(1, heads), skip_gain.reshape(1, heads), out_grad,
     )
+    return pl.pallas_call(
+        hand_over,
+        out_shape=tuple(jax.ShapeDtypeStruct(r.shape, r.dtype) for r in results),
+        in_specs=[hbm] * 4,
+        out_specs=(hbm,) * 4,
+        scratch_shapes=[dma((4, 4))],
+        compiler_params=pltpu.CompilerParams(vmem_limit_bytes=61 * 1024 * 1024),
+    )(*results)
 
 
 def solution(mesh):

time: 40.3 us -> 101 us (2.51)
  Pallas kernels: 34.7 us -> 100 us
  local copies, waits for them, and re-layouts: 4.75 us -> 0 us
    pallas_call x0 -> x1, Pallas kernels: none -> 66.8 us  [local(): pl.pallas_call(hand_over, out_shape=tuple((jax.ShapeDtypeStruct(r.shape,...]
    unnamed x10 -> x0, local copies, waits for them, and re-layouts: 4.75 us -> none
where the time goes in v3:
time: 101 us
  Pallas kernels  100 us (99%)
    pallas_call x1, Pallas kernels, local(): pl.pallas_call(hand_over, out_shape=tuple((jax.ShapeDtypeStruct(r.shape,...  66.8 us
    pallas_call x1, Pallas kernels, local(): pl.pallas_call(functools.partial(kernel, chips, zs, parts), out_shape=(ja...  33.7 us

profile of v3, /device:TPU:0, one launch (start us, length us, event | category | flops | bytes accessed | tf_op | source)
XLA Modules:
  0.0 101.1 jit_solution(5245277928179157929)
XLA Ops:
  0.6 33.7 %shard_map.102 = (bf16[256,2048]{1,0:T(8,128)(2,1)}, bf16[256,2048]{1,0:T(8,128)(2,1)}, f32[64,128]{1,0:T(8,128)}, f32[64,128]{1,0:T(8,128)}) custom-call(bf16[256,2048]{1,0:T(8,128)(2,1)} %x_hbm.1, bf16[64,128]{1,0:T(8,128)(2,1)} %b_hbm.1, bf16[64,128]{1,0:T(8,128)(2,1)} %c_hbm.1, s32[32,256]{1,0:T(8,128)} %codes_hbm.1, f32[1,32]{1,0:T(1,128)} %bitcast.2, ...), custom_call_target="tpu_custom_call" | custom-call | tf_op jit(solution)/shard_map/pallas_call | solution.py:378
  34.4 66.8 %shard_map.103 = (bf16[256,2048]{1,0:T(8,128)(2,1)}, bf16[256,2048]{1,0:T(8,128)(2,1)}, f32[64,128]{1,0:T(8,128)}, f32[64,128]{1,0:T(8,128)}) custom-call(bf16[256,2048]{1,0:T(8,128)(2,1)} %get-tuple-element.8.refs_0_, bf16[256,2048]{1,0:T(8,128)(2,1)} %get-tuple-element.9.refs_1_, f32[64,128]{1,0:T(8,128)} %get-tuple-element.10.refs_2_, ...), custom_call_target="tpu_custom_call" | custom-call | tf_op jit(solution)/shard_map/pallas_call | solution.py:440

commit v4 on v3

--- a/solution.py
+++ b/solution.py
@@ -31,7 +31,7 @@
 
 
 def kernel(
-    chips, zs, parts,
+    chips, zs, cuts,
     x_hbm, b_hbm, c_hbm, codes_hbm, rate_hbm, gain_hbm, g_hbm,
     out_hbm, ig_hbm, gb_ref, gc_ref,
     out_ref, ig_ref, x_ref, g_ref, codes_ref, rate_ref, gain_ref,
@@ -46,7 +46,7 @@
     rows, state = b_hbm.shape
     subs = tokens // SUB
     half = width // 2
-    size = half // parts
+    parts = len(cuts)
     seq = lax.axis_index("seq")
     z = lax.axis_index("head")
     chip = seq // 2
@@ -132,7 +132,7 @@
         return slice(a * SUB, (a + 1) * SUB)
 
     def chunk(h, k):
-        return slice(h * half + k * size, h * half + (k + 1) * size)
+        return slice(h * half + cuts[k][0], h * half + cuts[k][1])
 
     def root(a, lanes):
         return u_s[(a + 1) * SUB - 1 : (a + 1) * SUB, lanes]
@@ -147,8 +147,7 @@
             ug_s[:, lanes] = (u * g_ref[:, lanes].astype(F32)).astype(BF16)
             vx_s[:, lanes] = (vs * x_ref[:, lanes].astype(F32)).astype(BF16)
 
-    early = parts
-    for k in range(early):
+    for k in range(parts):
         factors(k)
     for each in gathers:
         each.wait()
@@ -158,7 +157,7 @@
     c_flip = c_all.astype(F32).T.astype(BF16)
 
     sib_copies = [
-        copy(pa.at[other, k], pc.at[core, k], s_send.at[k], s_recv.at[k], sib)
+        copy(pa.at[other, :, :, chunk(0, k)], pc.at[core, :, :, chunk(0, k)], s_send.at[k], s_recv.at[k], sib)
         for k in range(parts)
     ]
 
@@ -178,15 +177,15 @@
                     p_dev = (r * r) * p_dev + ps
                     a_dev = a_dev + total * ad
                     total = total * (r * r)
-            pa[h, k, 0] = p_dev
-            pa[h, k, 1] = a_dev
+            pa[h, 0, :, chunk(0, k)] = p_dev
+            pa[h, 1, :, chunk(0, k)] = a_dev
         sib_copies[k].start()
-        pc[core, k] = pa[core, k]
+        pc[core, :, :, chunk(0, k)] = pa[core, :, :, chunk(0, k)]
 
     to_chips = {}
 
     def combine(k):
-        here = slice(k * size, (k + 1) * size)
+        here = chunk(0, k)
         if k == 0:
             to_sib.wait()
             qt[...] = dc[0, 0] * dc[1, 0]
@@ -195,11 +194,11 @@
                 each.start()
                 to_chips[d] = each
         sib_copies[k].wait()
-        qb[k, 0] = (dc[1, 0, :, here] * pc[0, k, 0] + pc[1, k, 0]).astype(BF16)
-        qb[k, 1] = (pc[0, k, 1] + dc[0, 0, :, here] * pc[1, k, 1]).astype(BF16)
+        qb[0, :, here] = (dc[1, 0, :, here] * pc[0, 0, :, here] + pc[1, 0, :, here]).astype(BF16)
+        qb[1, :, here] = (pc[0, 1, :, here] + dc[0, 0, :, here] * pc[1, 1, :, here]).astype(BF16)
         for d in range(1, chips):
             each = copy(
-                qb.at[k, (chip + d) // chips], rq.at[k, d - 1],
+                qb.at[(chip + d) // chips, :, here], rq.at[d - 1, :, here],
                 q_send.at[k, d - 1], q_recv.at[k, d - 1], chip_peer(d),
             )
             each.start()
@@ -207,8 +206,6 @@
 
     summarize(0)
     for k in range(1, parts):
-        if k >= early:
-            factors(k)
         summarize(k)
         combine(k - 1)
     combine(parts - 1)
@@ -228,48 +225,49 @@
         c_sums.append(split_dot(paired, b_a))
 
     back = [
-        copy(tmp.at[other, k], ef.at[core, k], e_send.at[k], e_recv.at[k], sib)
+        copy(tmp.at[other, :, :, chunk(0, k)], ef.at[core, :, :, chunk(0, k)], e_send.at[k], e_recv.at[k], sib)
         for k in range(parts)
     ]
 
     def enter(k):
-        here = slice(k * size, (k + 1) * size)
+        here = chunk(0, k)
         for d in range(1, chips):
             if k == 0:
                 to_chips[d].wait()
             to_chips[k, d].wait()
+        size = cuts[k][1] - cuts[k][0]
         e_in = jnp.zeros((state, size), F32)
         f_in = jnp.zeros((state, size), F32)
         reach = jnp.ones((1, size), F32)
         for d in range(1, chips):
-            e_in = e_in + jnp.where(chip >= d, reach, 0.0) * rq[k, d - 1].astype(F32)
+            e_in = e_in + jnp.where(chip >= d, reach, 0.0) * rq[d - 1, :, here].astype(F32)
             reach = reach * rt[d - 1, :, here]
         reach = jnp.ones((1, size), F32)
         for d in range(chips - 1, 0, -1):
-            f_in = f_in + jnp.where(chip < d, reach, 0.0) * rq[k, d - 1].astype(F32)
+            f_in = f_in + jnp.where(chip < d, reach, 0.0) * rq[d - 1, :, here].astype(F32)
             reach = reach * rt[d - 1, :, here]
-        e_out = dc[0, 0, :, here] * e_in + pc[0, k, 0]
-        f_out = dc[1, 0, :, here] * f_in + pc[1, k, 1]
-        tmp[0, k, 0] = (dc[0, 1, :, here] * e_in).astype(BF16)
-        tmp[1, k, 0] = (dc[1, 1, :, here] * e_out).astype(BF16)
-        tmp[1, k, 1] = (dc[1, 2, :, here] * f_in).astype(BF16)
-        tmp[0, k, 1] = (dc[0, 2, :, here] * f_out).astype(BF16)
+        e_out = dc[0, 0, :, here] * e_in + pc[0, 0, :, here]
+        f_out = dc[1, 0, :, here] * f_in + pc[1, 1, :, here]
+        tmp[0, 0, :, here] = (dc[0, 1, :, here] * e_in).astype(BF16)
+        tmp[1, 0, :, here] = (dc[1, 1, :, here] * e_out).astype(BF16)
+        tmp[1, 1, :, here] = (dc[1, 2, :, here] * f_in).astype(BF16)
+        tmp[0, 1, :, here] = (dc[0, 2, :, here] * f_out).astype(BF16)
         back[k].start()
-        ef[core, k] = tmp[core, k]
+        ef[core, :, :, here] = tmp[core, :, :, here]
 
     def states(k):
         back[k].wait()
         es = {}
         for h in range(2):
             lanes = chunk(h, k)
-            es[h, 0, 0] = ef[h, k, 0]
-            es[h, subs - 1, 1] = ef[h, k, 1]
-            e = ef[h, k, 0].astype(F32)
+            es[h, 0, 0] = ef[h, 0, :, chunk(0, k)]
+            es[h, subs - 1, 1] = ef[h, 1, :, chunk(0, k)]
+            e = ef[h, 0, :, chunk(0, k)].astype(F32)
             for a in range(1, subs):
                 r = root(a, lanes)
                 e = r * (root(a - 1, lanes) * e + ps_s[a - 1, :, lanes])
                 es[h, a, 0] = e.astype(BF16)
-            f = ef[h, k, 1].astype(F32)
+            f = ef[h, 1, :, chunk(0, k)].astype(F32)
             for a in range(subs - 2, -1, -1):
                 r = root(a, lanes)
                 f = r * (root(a + 1, lanes) * f + as_s[a + 1, :, lanes])
@@ -315,13 +313,14 @@
             c_sums[a] = jnp.zeros((SUB, state), F32)
         return scatter(part, rpart, r_send, r_recv)
 
-    if parts < 3:
+    early = parts - 4
+    if early < 0:
         sent = scatter_early()
     enter(0)
     for k in range(1, parts):
         enter(k)
         es = states(k - 1)
-        if k == parts - 2:
+        if k - 1 == early:
             sent = scatter_early()
         outputs(k - 1, es)
     es = states(parts - 1)
@@ -346,19 +345,35 @@
         each.wait()
 
 
+def chunks(half):
+    units = half // 128
+    sizes = [1] * units
+    if units >= 4:
+        sizes = [1] + [2] * ((units - 2) // 2) + [1] * (1 + units % 2)
+    cuts, at = [], 0
+    for size in sizes:
+        cuts.append((at, at + 128 * size))
+        at += 128 * size
+    return cuts
+
+
 def hand_over(*refs):
-    count = (len(refs) - 1) // 2
-    sems = refs[-1]
-    copies = []
+    count = (len(refs) - 2) // 3
+    sems_in, sems_out = refs[-2:]
+    loads, stores = [], []
     for i in range(count):
-        src, dst = refs[i], refs[count + i]
+        src, dst, held = refs[i], refs[count + i], refs[2 * count + i]
         rows = src.shape[0] // 4
         for j in range(4):
             here = pl.ds(j * rows, rows)
-            copies.append(pltpu.make_async_copy(src.at[here], dst.at[here], sems.at[i, j]))
-    for each in copies:
+            loads.append(pltpu.make_async_copy(src.at[here], held.at[here], sems_in.at[i, j]))
+            stores.append(pltpu.make_async_copy(held.at[here], dst.at[here], sems_out.at[i, j]))
+    for each in loads:
         each.start()
-    for each in copies:
+    for load, store in zip(loads, stores):
+        load.wait()
+        store.start()
+    for each in stores:
         each.wait()
 
 
@@ -368,15 +383,15 @@
     heads = decay_codes.shape[0]
     subs = tokens // SUB
     half = width // 2
-    parts = max(1, min(4, half // 128))
-    size = half // parts
+    cuts = chunks(half)
+    parts = len(cuts)
     chips = lax.axis_size("seq") // 2
     zs = lax.axis_size("head")
     vmem = pl.BlockSpec(memory_space=pltpu.VMEM)
     hbm = pl.BlockSpec(memory_space=pltpu.MemorySpace.HBM)
     dma = pltpu.SemaphoreType.DMA
     results = pl.pallas_call(
-        functools.partial(kernel, chips, zs, parts),
+        functools.partial(kernel, chips, zs, cuts),
         out_shape=(
             jax.ShapeDtypeStruct((tokens, width), BF16),
             jax.ShapeDtypeStruct((tokens, width), BF16),
@@ -404,16 +419,16 @@
             pltpu.VMEM((1, width), F32),
             pltpu.VMEM((3 * heads, width), BF16),
             pltpu.VMEM((zs, 2, rows, state), BF16),
-            pltpu.VMEM((2, parts, 2, state, size), F32),
+            pltpu.VMEM((2, 2, state, half), F32),
             pltpu.VMEM((2, 3, 1, half), F32),
-            pltpu.VMEM((2, parts, 2, state, size), F32),
+            pltpu.VMEM((2, 2, state, half), F32),
             pltpu.VMEM((2, 3, 1, half), F32),
-            pltpu.VMEM((parts, 2, state, size), BF16),
+            pltpu.VMEM((2, state, half), BF16),
             pltpu.VMEM((1, half), F32),
-            pltpu.VMEM((parts, chips - 1, state, size), BF16),
+            pltpu.VMEM((chips - 1, state, half), BF16),
             pltpu.VMEM((chips - 1, 1, half), F32),
-            pltpu.VMEM((2, parts, 2, state, size), BF16),
-            pltpu.VMEM((2, parts, 2, state, size), BF16),
+            pltpu.VMEM((2, 2, state, half), BF16),
+            pltpu.VMEM((2, 2, state, half), BF16),
             pltpu.VMEM((zs, 2, rows, state), F32),
             pltpu.VMEM((zs - 1, 2, rows, state), F32),
             pltpu.VMEM((zs, 2, rows, state), F32),
@@ -442,7 +457,7 @@
         out_shape=tuple(jax.ShapeDtypeStruct(r.shape, r.dtype) for r in results),
         in_specs=[hbm] * 4,
         out_specs=(hbm,) * 4,
-        scratch_shapes=[dma((4, 4))],
+        scratch_shapes=[pltpu.VMEM(r.shape, r.dtype) for r in results] + [dma((4, 4)), dma((4, 4))],
         compiler_params=pltpu.CompilerParams(vmem_limit_bytes=61 * 1024 * 1024),
     )(*results)
 

time: 101 us -> 36 us (0.36)
  Pallas kernels: 100 us -> 35.2 us
    pallas_call x1, Pallas kernels: 66.8 us -> 2.55 us  [local(): pl.pallas_call(hand_over, out_shape=tuple((jax.ShapeDtypeStruct(r.shape,...]
    pallas_call x1, Pallas kernels: 33.7 us -> 32.7 us  [local(): pl.pallas_call(functools.partial(kernel, chips, zs, cuts), out_shape=(jax...]
where the time goes in v4:
time: 36 us; the launch traced here: 35.9 us
  Pallas kernels  35.2 us (98%)
  between operations  0.64 us (2%)
    pallas_call x1, Pallas kernels, local(): pl.pallas_call(functools.partial(kernel, chips, zs, cuts), out_shape=(jax...  32.7 us
    pallas_call x1, Pallas kernels, local(): pl.pallas_call(hand_over, out_shape=tuple((jax.ShapeDtypeStruct(r.shape,...  2.55 us

profile of v4, /device:TPU:0, one launch (start us, length us, event | category | flops | bytes accessed | tf_op | source)
XLA Modules:
  0.0 35.9 jit_solution(9729528882341435312)
XLA Ops:
  0.6 32.7 %shard_map.102 = (bf16[256,2048]{1,0:T(8,128)(2,1)}, bf16[256,2048]{1,0:T(8,128)(2,1)}, f32[64,128]{1,0:T(8,128)}, f32[64,128]{1,0:T(8,128)}) custom-call(bf16[256,2048]{1,0:T(8,128)(2,1)} %x_hbm.1, bf16[64,128]{1,0:T(8,128)(2,1)} %b_hbm.1, bf16[64,128]{1,0:T(8,128)(2,1)} %c_hbm.1, s32[32,256]{1,0:T(8,128)} %codes_hbm.1, f32[1,32]{1,0:T(1,128)} %bitcast.2, ...), custom_call_target="tpu_custom_call" | custom-call | tf_op jit(solution)/shard_map/pallas_call | solution.py:393
  33.3 2.6 %shard_map.103 = (bf16[256,2048]{1,0:T(8,128)(2,1)}, bf16[256,2048]{1,0:T(8,128)(2,1)}, f32[64,128]{1,0:T(8,128)}, f32[64,128]{1,0:T(8,128)}) custom-call(bf16[256,2048]{1,0:T(8,128)(2,1)} %get-tuple-element.8.refs_0_, bf16[256,2048]{1,0:T(8,128)(2,1)} %get-tuple-element.9.refs_1_, f32[64,128]{1,0:T(8,128)} %get-tuple-element.10.refs_2_, ...), custom_call_target="tpu_custom_call" | custom-call | tf_op jit(solution)/shard_map/pallas_call | solution.py:455

commit v5 on v4

--- a/solution.py
+++ b/solution.py
@@ -33,12 +33,12 @@
 def kernel(
     chips, zs, cuts,
     x_hbm, b_hbm, c_hbm, codes_hbm, rate_hbm, gain_hbm, g_hbm,
-    out_hbm, ig_hbm, gb_ref, gc_ref,
-    out_ref, ig_ref, x_ref, g_ref, codes_ref, rate_ref, gain_ref,
+    out_ref, ig_ref, gb_ref, gc_ref,
+    x_ref, g_ref, codes_ref, rate_ref, gain_ref,
     u_s, vs_s, ug_s, vx_s, od_s, gd_s, ps_s, as_s, gain_s, spread_s,
     bc, pa, dd, pc, dc, qb, qt, rq, rt, tmp, ef, part, rpart, late, lpart, rlate,
     l_sem, g_send, g_recv, d_send, d_recv, s_send, s_recv, e_send, e_recv,
-    q_send, q_recv, t_send, t_recv, r_send, r_recv, w_send, w_recv, o_sem,
+    q_send, q_recv, t_send, t_recv, r_send, r_recv, w_send, w_recv,
 ):
     tokens, width = x_ref.shape
     heads = codes_ref.shape[0]
@@ -81,15 +81,8 @@
     for d in range(1, chips):
         pl.semaphore_signal(barrier, inc=1, device_id=chip_peer(d), device_id_type=MESH)
     pl.semaphore_signal(barrier, inc=1, device_id=sib, device_id_type=MESH)
-    for each in loads[:5]:
+    for each in loads[:3]:
         each.wait()
-    pl.semaphore_wait(barrier, zs + chips - 1)
-    gathers = [
-        copy(bc.at[z], bc.at[z], g_send.at[d - 1], g_recv.at[d - 1], z_peer(d))
-        for d in range(1, zs)
-    ]
-    for each in gathers:
-        each.start()
 
     eye = lax.broadcasted_iota(jnp.int32, (heads, heads), 0) == lax.broadcasted_iota(
         jnp.int32, (heads, heads), 1
@@ -122,6 +115,16 @@
         dd[0, i] = end[:, :half]
         dd[1, i] = end[:, half:]
     spread_s[...] = jnp.concatenate([own.astype(F32)] * 3, axis=0).astype(BF16)
+    for each in loads[3:5]:
+        each.wait()
+    pl.semaphore_wait(barrier, zs + chips - 1)
+    gathers = [
+        copy(bc.at[z], bc.at[z], g_send.at[d - 1], g_recv.at[d - 1], z_peer(d))
+        for d in range(1, zs)
+    ]
+    for each in gathers:
+        each.start()
+
     to_sib = copy(dd.at[other], dc.at[core], d_send.at[0], d_recv.at[0], sib)
     to_sib.start()
     dc[core] = dd[core]
@@ -277,8 +280,6 @@
                 c_sums[a] += dot(ug_s[block(a), lanes], es[h, a, 0], ((1,), (1,)))
         return es
 
-    stores = []
-
     def outputs(k, es):
         for h in range(2):
             lanes = chunk(h, k)
@@ -291,10 +292,6 @@
                 grad = vs_s[block(a), lanes] * grad
                 grad = grad + gain_s[:, lanes] * g_ref[block(a), lanes].astype(F32)
                 ig_ref[block(a), lanes] = grad.astype(BF16)
-            for i, (src, dst) in enumerate([(out_ref, out_hbm), (ig_ref, ig_hbm)]):
-                each = pltpu.make_async_copy(src.at[:, lanes], dst.at[:, lanes], o_sem.at[k, h, i])
-                each.start()
-                stores.append(each)
 
     def scatter(src, dst, send, recv):
         copies = [
@@ -341,8 +338,6 @@
         gc = gc + rlate[d, 1].astype(F32)
     gb_ref[...] = gb
     gc_ref[...] = gc
-    for each in stores:
-        each.wait()
 
 
 def chunks(half):
@@ -358,22 +353,18 @@
 
 
 def hand_over(*refs):
-    count = (len(refs) - 2) // 3
-    sems_in, sems_out = refs[-2:]
-    loads, stores = [], []
+    count = (len(refs) - 1) // 2
+    sems = refs[-1]
+    copies = []
     for i in range(count):
-        src, dst, held = refs[i], refs[count + i], refs[2 * count + i]
+        src, dst = refs[i], refs[count + i]
         rows = src.shape[0] // 4
         for j in range(4):
             here = pl.ds(j * rows, rows)
-            loads.append(pltpu.make_async_copy(src.at[here], held.at[here], sems_in.at[i, j]))
-            stores.append(pltpu.make_async_copy(held.at[here], dst.at[here], sems_out.at[i, j]))
-    for each in loads:
+            copies.append(pltpu.make_async_copy(src.at[here], dst.at[here], sems.at[i, j]))
+    for each in copies:
         each.start()
-    for load, store in zip(loads, stores):
-        load.wait()
-        store.start()
-    for each in stores:
+    for each in copies:
         each.wait()
 
 
@@ -393,16 +384,14 @@
     results = pl.pallas_call(
         functools.partial(kernel, chips, zs, cuts),
         out_shape=(
-            jax.ShapeDtypeStruct((tokens, width), BF16),
-            jax.ShapeDtypeStruct((tokens, width), BF16),
-            jax.ShapeDtypeStruct((rows, state), F32),
-            jax.ShapeDtypeStruct((rows, state), F32),
+            pltpu.MemorySpace.VMEM((tokens, width), BF16),
+            pltpu.MemorySpace.VMEM((tokens, width), BF16),
+            pltpu.MemorySpace.VMEM((rows, state), F32),
+            pltpu.MemorySpace.VMEM((rows, state), F32),
         ),
         in_specs=[hbm] * 7,
-        out_specs=(hbm, hbm, vmem, vmem),
+        out_specs=(vmem,) * 4,
         scratch_shapes=[
-            pltpu.VMEM((tokens, width), BF16),
-            pltpu.VMEM((tokens, width), BF16),
             pltpu.VMEM((tokens, width), BF16),
             pltpu.VMEM((tokens, width), BF16),
             pltpu.VMEM(decay_codes.shape, jnp.int32),
@@ -443,10 +432,9 @@
             dma((chips - 1,)), dma((chips - 1,)),
             dma((zs - 1,)), dma((zs - 1,)),
             dma((zs - 1,)), dma((zs - 1,)),
-            dma((parts, 2, 2)),
         ],
         compiler_params=pltpu.CompilerParams(
-            collective_id=0, has_side_effects=True, vmem_limit_bytes=61 * 1024 * 1024
+            collective_id=0, has_side_effects=True, vmem_limit_bytes=58 * 1024 * 1024
         ),
     )(
         x_in, b_in, c_in, decay_codes,
@@ -455,10 +443,10 @@
     return pl.pallas_call(
         hand_over,
         out_shape=tuple(jax.ShapeDtypeStruct(r.shape, r.dtype) for r in results),
-        in_specs=[hbm] * 4,
+        in_specs=[vmem] * 4,
         out_specs=(hbm,) * 4,
-        scratch_shapes=[pltpu.VMEM(r.shape, r.dtype) for r in results] + [dma((4, 4)), dma((4, 4))],
-        compiler_params=pltpu.CompilerParams(vmem_limit_bytes=61 * 1024 * 1024),
+        scratch_shapes=[dma((4, 4))],
+        compiler_params=pltpu.CompilerParams(vmem_limit_bytes=4 * 1024 * 1024),
     )(*results)
 
 

time: 36 us -> 34.1 us (0.947)
  Pallas kernels: 35.2 us -> 33.3 us
    pallas_call x1, Pallas kernels: 2.55 us -> 1.46 us  [local(): pl.pallas_call(hand_over, out_shape=tuple((jax.ShapeDtypeStruct(r.shape,...]
    pallas_call x1, Pallas kernels: 32.7 us -> 31.8 us  [local(): pl.pallas_call(functools.partial(kernel, chips, zs, cuts), out_shape=(plt...]
where the time goes in v5:
time: 34.1 us; the launch traced here: 33.9 us
  Pallas kernels  33.3 us (98%)
  between operations  0.64 us (2%)
    pallas_call x1, Pallas kernels, local(): pl.pallas_call(functools.partial(kernel, chips, zs, cuts), out_shape=(plt...  31.8 us
    pallas_call x1, Pallas kernels, local(): pl.pallas_call(hand_over, out_shape=tuple((jax.ShapeDtypeStruct(r.shape,...  1.46 us

profile of v5, /device:TPU:0, one launch (start us, length us, event | category | flops | bytes accessed | tf_op | source)
XLA Modules:
  0.0 33.9 jit_solution(785324370531950305)
XLA Ops:
  0.6 31.8 %shard_map.102 = (bf16[256,2048]{1,0:T(8,128)(2,1)S(1)}, bf16[256,2048]{1,0:T(8,128)(2,1)S(1)}, f32[64,128]{1,0:T(8,128)S(1)}, f32[64,128]{1,0:T(8,128)S(1)}) custom-call(bf16[256,2048]{1,0:T(8,128)(2,1)} %x_hbm.1, bf16[64,128]{1,0:T(8,128)(2,1)} %b_hbm.1, bf16[64,128]{1,0:T(8,128)(2,1)} %c_hbm.1, s32[32,256]{1,0:T(8,128)} %codes_hbm.1, f32[1,32]{1,0:T(1,128)} %bitcast.2, ...), custom_call_target="tpu_custom_call" | custom-call | tf_op jit(solution)/shard_map/pallas_call | solution.py:384
  32.5 1.5 %shard_map.103 = (bf16[256,2048]{1,0:T(8,128)(2,1)}, bf16[256,2048]{1,0:T(8,128)(2,1)}, f32[64,128]{1,0:T(8,128)}, f32[64,128]{1,0:T(8,128)}) custom-call(bf16[256,2048]{1,0:T(8,128)(2,1)S(1)} %get-tuple-element.8.refs_0_, bf16[256,2048]{1,0:T(8,128)(2,1)S(1)} %get-tuple-element.9.refs_1_, f32[64,128]{1,0:T(8,128)S(1)} %get-tuple-element.10.refs_2_, ...), custom_call_target="tpu_custom_call" | custom-call | tf_op jit(solution)/shard_map/pallas_call | solution.py:443

commit v6 on v5

--- a/solution.py
+++ b/solution.py
@@ -311,6 +311,7 @@
         return scatter(part, rpart, r_send, r_recv)
 
     early = parts - 4
+    held = []
     if early < 0:
         sent = scatter_early()
     enter(0)
@@ -319,13 +320,17 @@
         es = states(k - 1)
         if k - 1 == early:
             sent = scatter_early()
-        outputs(k - 1, es)
-    es = states(parts - 1)
+        if k - 1 <= early:
+            outputs(k - 1, es)
+        else:
+            held.append((k - 1, es))
+    held.append((parts - 1, states(parts - 1)))
     late[:, 0] = jnp.concatenate(b_sums, axis=0).reshape(zs, rows, state)
     late[:, 1] = jnp.concatenate(c_sums, axis=0).reshape(zs, rows, state)
     lpart[...] = late[...].astype(BF16)
     sent_late = scatter(lpart, rlate, w_send, w_recv)
-    outputs(parts - 1, es)
+    for k, es in held:
+        outputs(k, es)
     gb = part[z, 0] + late[z, 0]
     gc = part[z, 1] + late[z, 1]
     for d in range(zs - 1):

time: 34.1 us -> 34.1 us (level)
  no operation moved by 1% of the time
where the time goes in v6:
time: 34.1 us; the launch traced here: 33.9 us
  Pallas kernels  33.3 us (98%)
  between operations  0.64 us (2%)
    pallas_call x1, Pallas kernels, local(): pl.pallas_call(functools.partial(kernel, chips, zs, cuts), out_shape=(plt...  31.8 us
    pallas_call x1, Pallas kernels, local(): pl.pallas_call(hand_over, out_shape=tuple((jax.ShapeDtypeStruct(r.shape,...  1.46 us

profile of v6, /device:TPU:0, one launch (start us, length us, event | category | flops | bytes accessed | tf_op | source)
XLA Modules:
  0.0 33.9 jit_solution(16108625955295889720)
XLA Ops:
  0.6 31.8 %shard_map.102 = (bf16[256,2048]{1,0:T(8,128)(2,1)S(1)}, bf16[256,2048]{1,0:T(8,128)(2,1)S(1)}, f32[64,128]{1,0:T(8,128)S(1)}, f32[64,128]{1,0:T(8,128)S(1)}) custom-call(bf16[256,2048]{1,0:T(8,128)(2,1)} %x_hbm.1, bf16[64,128]{1,0:T(8,128)(2,1)} %b_hbm.1, bf16[64,128]{1,0:T(8,128)(2,1)} %c_hbm.1, s32[32,256]{1,0:T(8,128)} %codes_hbm.1, f32[1,32]{1,0:T(1,128)} %bitcast.2, ...), custom_call_target="tpu_custom_call" | custom-call | tf_op jit(solution)/shard_map/pallas_call | solution.py:389
  32.5 1.5 %shard_map.103 = (bf16[256,2048]{1,0:T(8,128)(2,1)}, bf16[256,2048]{1,0:T(8,128)(2,1)}, f32[64,128]{1,0:T(8,128)}, f32[64,128]{1,0:T(8,128)}) custom-call(bf16[256,2048]{1,0:T(8,128)(2,1)S(1)} %get-tuple-element.8.refs_0_, bf16[256,2048]{1,0:T(8,128)(2,1)S(1)} %get-tuple-element.9.refs_1_, f32[64,128]{1,0:T(8,128)S(1)} %get-tuple-element.10.refs_2_, ...), custom_call_target="tpu_custom_call" | custom-call | tf_op jit(solution)/shard_map/pallas_call | solution.py:448

commit v7 on v6

--- a/solution.py
+++ b/solution.py
@@ -348,8 +348,8 @@
 def chunks(half):
     units = half // 128
     sizes = [1] * units
-    if units >= 4:
-        sizes = [1] + [2] * ((units - 2) // 2) + [1] * (1 + units % 2)
+    if units >= 6:
+        sizes = [1, 1] + [2] * ((units - 4) // 2) + [1] * (2 + units % 2)
     cuts, at = [], 0
     for size in sizes:
         cuts.append((at, at + 128 * size))

time: 34.1 us -> 35.1 us (1.029)
  Pallas kernels: 33.3 us -> 34.3 us
    pallas_call x1, Pallas kernels: 31.8 us -> 32.8 us  [local(): pl.pallas_call(functools.partial(kernel, chips, zs, cuts), out_shape=(plt...]
where the time goes in v7:
time: 35.1 us; the launch traced here: 34.9 us
  Pallas kernels  34.3 us (98%)
  between operations  0.64 us (2%)
    pallas_call x1, Pallas kernels, local(): pl.pallas_call(functools.partial(kernel, chips, zs, cuts), out_shape=(plt...  32.8 us
    pallas_call x1, Pallas kernels, local(): pl.pallas_call(hand_over, out_shape=tuple((jax.ShapeDtypeStruct(r.shape,...  1.46 us

profile of v7, /device:TPU:0, one launch (start us, length us, event | category | flops | bytes accessed | tf_op | source)
XLA Modules:
  0.0 34.9 jit_solution(5079822304523104258)
XLA Ops:
  0.6 32.8 %shard_map.102 = (bf16[256,2048]{1,0:T(8,128)(2,1)S(1)}, bf16[256,2048]{1,0:T(8,128)(2,1)S(1)}, f32[64,128]{1,0:T(8,128)S(1)}, f32[64,128]{1,0:T(8,128)S(1)}) custom-call(bf16[256,2048]{1,0:T(8,128)(2,1)} %x_hbm.1, bf16[64,128]{1,0:T(8,128)(2,1)} %b_hbm.1, bf16[64,128]{1,0:T(8,128)(2,1)} %c_hbm.1, s32[32,256]{1,0:T(8,128)} %codes_hbm.1, f32[1,32]{1,0:T(1,128)} %bitcast.2, ...), custom_call_target="tpu_custom_call" | custom-call | tf_op jit(solution)/shard_map/pallas_call | solution.py:389
  33.4 1.5 %shard_map.103 = (bf16[256,2048]{1,0:T(8,128)(2,1)}, bf16[256,2048]{1,0:T(8,128)(2,1)}, f32[64,128]{1,0:T(8,128)}, f32[64,128]{1,0:T(8,128)}) custom-call(bf16[256,2048]{1,0:T(8,128)(2,1)S(1)} %get-tuple-element.8.refs_0_, bf16[256,2048]{1,0:T(8,128)(2,1)S(1)} %get-tuple-element.9.refs_1_, f32[64,128]{1,0:T(8,128)S(1)} %get-tuple-element.10.refs_2_, ...), custom_call_target="tpu_custom_call" | custom-call | tf_op jit(solution)/shard_map/pallas_call | solution.py:448
